TPU v7x, 128 devices: a whole 4x4x4 slice. The times are simulated.
128 devices in a mesh: chord: 8 (over z_hi, y), span: 16 (over x, z_lo, core).
Axes of the slice: x: 4, y: 4, z: 4 (z_hi: 2, z_lo: 2; z = z_hi * 2 + z_lo), core: 2. Of those that a mesh axis runs over, the one named last changes fastest.
Arguments:
- flow_state: float32 [6, 12, 64, 2048], P(None, None, 'chord', 'span'), may hold values from -0.25 to 3, as said below
- displacement: float32 [3, 12, 64, 2048], P(None, None, 'chord', 'span'), may hold values from -0.2 to 0.2
- wall_distance: float32 [12, 64, 2048], P(None, 'chord', 'span'), may hold values from 0.5 to 4
- face_codes: int32 [64, 2048], P('chord', 'span'), may hold values from 0 to 2
- cost_gradient: float32 [6, 12, 64, 2048], P(None, None, 'chord', 'span'), may hold values from -20 to 20
Outputs:
- basis_next: float32 [6, 12, 64, 2048], P(None, None, 'chord', 'span')
- hessenberg: float32 [5], replicated
Inputs may be any that keep to these rules, and one draw needn't show every extreme that they name: `flow_state`: density lies in 0.8 to 1.2, each momentum in -0.25 to 0.25, energy in 2 to 3, and the last variable is the density times a value in 0.02 to 0.2. `face_codes`: 0 slip wall, 1 no-slip wall, 2 far field.
All inputs are finite; a program needn't handle non-finite values.
Results may differ from a plain program's by a relative error of at most 0.0003.
Values sent between devices are 32-bit elements; how exact they have to be, the bound alone decides.
A program may use at most 128 MiB of HBM per device.

v0:
```python
import jax
import jax.numpy as jnp
from jax import lax
from jax.sharding import PartitionSpec as P

HEAT_RATIO = 1.4
GAMMA_LESS = 0.4
VISCOSITY = 0.2
HEAT_FACTOR = 1.4 / (0.4 * 0.72)
CB_ONE = 0.1355
CW_ONE = 3.239
CV_CUBE = 7.1 * 7.1 * 7.1
TURB_SIGMA = 2.0 / 3.0
LIMIT_EPS = 0.01
NORM_EPS = 1e-06
FREESTREAM = (1.0, 0.2, 0.0, 0.05, 2.5, 0.1)
SLIP_SIGNS = (1.0, 1.0, 1.0, -1.0, 1.0, 1.0)
WALL_SIGNS = (1.0, -1.0, -1.0, -1.0, 1.0, -1.0)


def passed_along(block, axis, distance):
    devices = range(lax.axis_size(axis))
    route = [((i - distance) % len(devices), i) for i in devices]
    return lax.ppermute(block, axis, route)


def extended(cells, sides, width):
    for axis, dim in sides:
        count = lax.axis_size(axis)
        head = lax.slice_in_dim(cells, 0, width, axis=dim)
        tail = lax.slice_in_dim(cells, cells.shape[dim] - width, cells.shape[dim], axis=dim)
        cells = jnp.concatenate(
            [
                lax.ppermute(tail, axis, [(i, (i + 1) % count) for i in range(count)]),
                cells,
                lax.ppermute(head, axis, [((i + 1) % count, i) for i in range(count)]),
            ],
            axis=dim,
        )
    return cells


def limiter(upwind, downwind):
    return (
        (downwind * downwind + LIMIT_EPS) * upwind + (upwind * upwind + LIMIT_EPS) * downwind
    ) / (upwind * upwind + downwind * downwind + 2.0 * LIMIT_EPS)


def primitive(state):
    density = state[0]
    velocity = state[1:4] / density
    pressure = GAMMA_LESS * (state[4] - 0.5 * density * jnp.sum(velocity * velocity, axis=0))
    return (density, velocity, pressure)


def normal_flux(state, normal):
    density, velocity, pressure = primitive(state)
    normal_speed = jnp.sum(velocity * normal, axis=0)
    momentum = state[1:4] * normal_speed + pressure * normal
    return jnp.concatenate(
        [
            (state[0] * normal_speed)[None],
            momentum,
            ((state[4] + pressure) * normal_speed)[None],
            (state[5] * normal_speed)[None],
        ],
        axis=0,
    )


def face_flux(before, left_cell, right_cell, beyond, direction):
    offsets = right_cell[6:] - left_cell[6:]
    unit_vector = jnp.array(
        [1.0 if member == direction else 0.0 for member in range(3)], jnp.float32
    )
    spacing = offsets + unit_vector.reshape((3,) + (1,) * (offsets.ndim - 1))
    distance = jnp.sqrt(jnp.sum(spacing * spacing, axis=0))
    normal = spacing / distance
    weight = 1.0 / distance
    left_state = left_cell[:6] + 0.5 * limiter(
        left_cell[:6] - before[:6], right_cell[:6] - left_cell[:6]
    )
    right_state = right_cell[:6] - 0.5 * limiter(
        right_cell[:6] - left_cell[:6], beyond[:6] - right_cell[:6]
    )
    mean_density, mean_velocity, mean_pressure = primitive(0.5 * (left_state + right_state))
    wave_speed = jnp.abs(jnp.sum(mean_velocity * normal, axis=0)) + jnp.sqrt(
        HEAT_RATIO * mean_pressure / mean_density
    )
    convective = 0.5 * (
        normal_flux(left_state, normal) + normal_flux(right_state, normal)
    ) - 0.5 * wave_speed * (right_state - left_state)
    density_left, velocity_left, pressure_left = primitive(left_cell[:6])
    density_right, velocity_right, pressure_right = primitive(right_cell[:6])
    turb_left = left_cell[5] / density_left
    turb_right = right_cell[5] / density_right
    face_density = 0.5 * (density_left + density_right)
    face_turb = 0.5 * (turb_left + turb_right)
    visc_ratio = face_density * face_turb / VISCOSITY
    ratio_cube = visc_ratio * visc_ratio * visc_ratio
    effective = (
        VISCOSITY + face_density * face_turb * ratio_cube / (ratio_cube + CV_CUBE)
    ) * weight
    energy_jump = HEAT_FACTOR * (
        pressure_right / density_right - pressure_left / density_left
    ) + 0.5 * (
        jnp.sum(velocity_right * velocity_right, axis=0)
        - jnp.sum(velocity_left * velocity_left, axis=0)
    )
    turb_flux = (
        (VISCOSITY + face_density * face_turb) / TURB_SIGMA * weight * (turb_right - turb_left)
    )
    viscous = jnp.concatenate(
        [
            jnp.zeros_like(face_density)[None],
            -effective * (velocity_right - velocity_left),
            (-effective * energy_jump)[None],
            (-turb_flux)[None],
        ],
        axis=0,
    )
    return convective + viscous


def boundary_ghost(state, face_codes):
    slip_state = jnp.array(SLIP_SIGNS, jnp.float32)[:, None, None] * state
    wall_state = jnp.array(WALL_SIGNS, jnp.float32)[:, None, None] * state
    far_state = jnp.broadcast_to(jnp.array(FREESTREAM, jnp.float32)[:, None, None], state.shape)
    code_plane = face_codes[None]
    return jnp.where(code_plane == 0, slip_state, jnp.where(code_plane == 1, wall_state, far_state))


def axis_pullback(window, face_cot, grid_dim):
    metric_part = window[6:]
    extent = window.shape[grid_dim]

    def fluxes(flow_part):
        full_state = jnp.concatenate([flow_part, metric_part], axis=0)
        pieces = [
            lax.slice_in_dim(full_state, offset, offset + extent - 3, axis=grid_dim)
            for offset in range(4)
        ]
        return face_flux(pieces[0], pieces[1], pieces[2], pieces[3], grid_dim - 2)

    unused, pullback = jax.vjp(fluxes, window[:6])
    return pullback(face_cot)[0]


def column_pullback(block_cells, adjoint, face_codes, wall_distance):
    metric_part = block_cells[6:]
    layers = block_cells.shape[1]

    def column_terms(flow_part):
        ghost_near = boundary_ghost(flow_part[:, 0], face_codes)
        ghost_far = boundary_ghost(flow_part[:, 1], face_codes)
        far_state = jnp.broadcast_to(
            jnp.array(FREESTREAM, jnp.float32)[:, None, None], ghost_near.shape
        )
        flow_layers = jnp.concatenate(
            [
                ghost_far[:, None],
                ghost_near[:, None],
                flow_part,
                far_state[:, None],
                far_state[:, None],
            ],
            axis=1,
        )
        metric = jnp.concatenate(
            [
                metric_part[:, 1:2],
                metric_part[:, 0:1],
                metric_part,
                metric_part[:, -1:],
                metric_part[:, -1:],
            ],
            axis=1,
        )
        full_state = jnp.concatenate([flow_layers, metric], axis=0)
        pieces = [
            lax.slice_in_dim(full_state, offset, offset + layers + 1, axis=1) for offset in range(4)
        ]
        fluxes = face_flux(pieces[0], pieces[1], pieces[2], pieces[3], 2)
        density = flow_part[0]
        velocity = flow_part[1:4] / density
        turbulence = flow_part[5] / density
        shear_rate = jnp.sqrt(jnp.sum(velocity * velocity, axis=0) + 0.01) / wall_distance
        scaled = turbulence / wall_distance
        source = density * (CB_ONE * shear_rate * turbulence - CW_ONE * scaled * scaled)
        return (fluxes, source)

    zero_layers = jnp.zeros_like(adjoint[:, :2])
    padded = jnp.concatenate([zero_layers, adjoint, zero_layers], axis=1)
    face_cot = padded[:, 1 : layers + 2] - padded[:, 2 : layers + 3]
    unused, pullback = jax.vjp(column_terms, block_cells[:6])
    return pullback((face_cot, -adjoint[5]))[0]


def chord_return(state_rims, adjoint):
    cells_along = adjoint.shape[2]
    window = state_rims[:, :, 1:, 2:-2]
    ahead_layer = passed_along(adjoint[:, :, :1, :], "chord", -1)
    joined = jnp.concatenate([adjoint, ahead_layer], axis=2)
    result = axis_pullback(window, joined[:, :, :-1] - joined[:, :, 1:], 2)
    own_part = result[:, :, 1 : cells_along + 1]
    from_above = passed_along(result[:, :, :1], "chord", -1)
    from_below = passed_along(result[:, :, cells_along + 1 :], "chord", 1)
    own_part = own_part.at[:, :, cells_along - 1 :].add(from_above)
    return own_part.at[:, :, :2].add(from_below)


def span_return(state_rims, adjoint):
    cells_along = adjoint.shape[3]
    window = state_rims[:, :, 2:-2, 1:]
    ahead_layer = passed_along(adjoint[:, :, :, :1], "span", -1)
    joined = jnp.concatenate([adjoint, ahead_layer], axis=3)
    result = axis_pullback(window, joined[:, :, :, :-1] - joined[:, :, :, 1:], 3)
    own_part = result[:, :, :, 1 : cells_along + 1]
    from_above = passed_along(result[:, :, :, :1], "span", -1)
    from_below = passed_along(result[:, :, :, cells_along + 1 :], "span", 1)
    own_part = own_part.at[:, :, :, cells_along - 1 :].add(from_above)
    return own_part.at[:, :, :, :2].add(from_below)


def on_device(flow_state, displacement, wall_distance, face_codes, cost_gradient):
    state = jnp.concatenate([flow_state, displacement], axis=0)
    entries = float(cost_gradient.size * lax.axis_size("chord") * lax.axis_size("span"))
    state_rims = extended(state, (("chord", 2), ("span", 3)), 2)

    def product(adjoint):
        chord_part = chord_return(state_rims, adjoint)
        span_part = span_return(state_rims, adjoint)
        return chord_part + span_part + column_pullback(state, adjoint, face_codes, wall_distance)

    def orthogonal(mapped, basis_set):
        partial_value = jnp.stack(
            [jnp.sum(mapped * basis_set[member]) for member in range(basis_set.shape[0])]
        )
        coefficients = lax.psum(partial_value, ("chord", "span")) / entries
        for member in range(basis_set.shape[0]):
            mapped = mapped - coefficients[member] * basis_set[member]
        length = jnp.sqrt(
            lax.psum(jnp.sum(mapped * mapped), ("chord", "span")) / entries + NORM_EPS
        )
        return (mapped / length, coefficients, length)

    seed_total = lax.psum(jnp.sum(cost_gradient * cost_gradient), ("chord", "span"))
    leading = cost_gradient / jnp.sqrt(seed_total / entries + NORM_EPS)
    second, upper_one, length_one = orthogonal(product(leading), leading[None])
    basis_next, upper_two, length_two = orthogonal(product(second), jnp.stack([leading, second]))
    hessenberg = jnp.stack([upper_one[0], length_one, upper_two[0], upper_two[1], length_two])
    return (basis_next, hessenberg)


def solution(mesh):
    return jax.shard_map(
        on_device,
        mesh=mesh,
        in_specs=(
            P(None, None, "chord", "span"),
            P(None, None, "chord", "span"),
            P(None, "chord", "span"),
            P("chord", "span"),
            P(None, None, "chord", "span"),
        ),
        out_specs=(P(None, None, "chord", "span"), P()),
        check_vma=False,
    )
```

profile of v0, /device:TPU:1, one launch (start us, length us, event | category | flops | bytes accessed | tf_op | source)
XLA Modules:
  0.0 498.5 jit_solution(15993410784577422127)
XLA Ops:
  0.7 1.1 constant_dynamic-update-slice_fusion.1
  2.8 6.9 %collective-permute-start = (f32[9,12,2,128]{3,2,1,0:T(2,128)S(1)}, f32[9,12,2,128]{3,2,1,0:T(2,128)S(1)}, u32[]{:S(2)}, u32[]{:S(2)}) collective-permute-start(f32[9,12,2,128]{3,2,1,0:T(2,128)S(1)} %get-tuple-element.520), channel_id=1, source_target_pairs={{16,0},{32,16},{48,32},{64,48},{80,64},{96,80},{112,96},{0,112},{1... | collective-permute-start | bytes 331784 | tf_op jit(solution)/shard_map/ppermute | solution.py:36
  9.7 1.6 multiply_reduce_fusion.11
  11.4 67.0 %psum.35 = f32[]{:T(128)} all-reduce(f32[]{:T(128)} %multiply_reduce_fusion.11), channel_id=1, replica_groups=mesh['chord'=8,'span'=16] {'chord','span'}, use_global_device_ids=true, to_apply=%region_6.0 | all-reduce | flops 1 | bytes 8 | tf_op jit(solution)/shard_map/psum | solution.py:247
  81.7 1.9 collective-permute-start.2
  83.8 2.1 multiply_reduce_fusion.1
  93.7 3.1 multiply_reduce_fusion.10
  98.4 1.5 fusion.521
  99.9 1.9 copy.105
  101.8 1.7 collective-permute-start.5
  103.5 2.5 copy.106
  107.7 1.7 copy.102
  109.3 2.4 pad_maximum_fusion
  111.7 2.6 copy.104
  114.3 3.5 multiply_reduce_fusion.9
  133.8 1.2 multiply_reduce_fusion.69
  135.0 1.6 add_divide_fusion.4
  136.7 1.6 divide_bitcast_fusion.3
  138.3 1.6 multiply_reduce_fusion.87
  139.9 1.6 fusion.312
  142.4 1.5 add_divide_fusion.5
  148.1 1.1 fusion.469
  149.2 1.3 fusion.470
  153.7 1.2 collective-permute-start.8
  157.8 5.1 %collective-permute-start.3 = (f32[6,12,1,128]{3,2,1,0:T(1,128)}, f32[6,12,1,128]{3,2,1,0:T(1,128)}, u32[]{:S(2)}, u32[]{:S(2)}) collective-permute-start(f32[6,12,1,128]{3,2,1,0:T(1,128)} %pad_add_fusion.39), channel_id=1, source_target_pairs={{16,0},{32,16},{48,32},{64,48},{80,64},{96,80},{112,96},{0,112},{1... | collective-permute-start | bytes 110600 | tf_op jit(solution)/shard_map/ppermute | solution.py:24
  164.4 6.9 %scatter-add.30 = f32[6,12,8,128]{3,2,1,0:T(8,128)} dynamic-update-slice(f32[6,12,8,128]{3,2,1,0:T(8,128)} %slice.1089, f32[6,12,8,1]{3,2,1,0:T(8,128)} %slice_add_fusion.5, s32[]{:T(128)} %constant.295.clone.1, s32[]{:T(128)} %constant.295.clone.1, s32[]{:T(128)} %constant.295.clone.1, s32[]{:T(128)} %constant.297.clone.1) | dynamic-update-slice | bytes 4612 | tf_op jit(solution)/shard_map/scatter-add | solution.py:221
  171.3 1.8 slice_add_fusion.4
  173.1 1.8 scatter-add.31
  174.9 1.7 add_add_fusion.97
  176.6 1.8 scatter-add.26
  178.4 1.7 fusion.52
  180.1 2.0 multiply_reduce_fusion.8
  182.0 66.1 %psum.36 = f32[1]{0:T(128)} all-reduce(f32[1]{0:T(128)} %bitcast.130), channel_id=1, replica_groups=mesh['chord'=8,'span'=16] {'chord','span'}, use_global_device_ids=true, to_apply=%region_65.0 | all-reduce | flops 1 | bytes 8 | tf_op jit(solution)/shard_map/psum | solution.py:239
  249.5 64.2 %psum.37 = f32[]{:T(128)} all-reduce(f32[]{:T(128)} %multiply_reduce_fusion.7), channel_id=1, replica_groups=mesh['chord'=8,'span'=16] {'chord','span'}, use_global_device_ids=true, to_apply=%region_67.0 | all-reduce | flops 1 | bytes 8 | tf_op jit(solution)/shard_map/psum | solution.py:243
  314.6 1.1 multiply_reduce_fusion
  315.9 1.0 collective-permute-start.13
  316.9 1.2 collective-permute-start.10
  331.5 1.0 multiply_reduce_fusion.46
  342.1 1.2 fusion.433
  343.2 1.1 fusion.430
  345.8 2.3 collective-permute-start.14
  349.2 5.3 %collective-permute-start.11 = (f32[6,12,1,128]{3,2,1,0:T(1,128)S(1)}, f32[6,12,1,128]{3,2,1,0:T(1,128)S(1)}, u32[]{:S(2)}, u32[]{:S(2)}) collective-permute-start(f32[6,12,1,128]{3,2,1,0:T(1,128)S(1)} %pad_add_fusion.38), channel_id=1, source_target_pairs={{16,0},{32,16},{48,32},{64,48},{80,64},{96,80},{112,96},{0,112},{1... | collective-permute-start | bytes 110600 | tf_op jit(solution)/shard_map/ppermute | solution.py:24
  354.5 5.2 %scatter-add.36 = f32[6,12,8,128]{3,2,1,0:T(8,128)S(1)} dynamic-update-slice(f32[6,12,8,128]{3,2,1,0:T(8,128)S(1)} %slice.1126, f32[6,12,8,1]{3,2,1,0:T(8,128)S(1)} %slice_add_fusion.2, s32[]{:T(128)} %constant.295.clone.1, s32[]{:T(128)} %constant.295.clone.1, s32[]{:T(128)} %constant.295.clone.1, s32[]{:T(128)} %constant.297.clone.1) | dynamic-update-slice | bytes 4612 | tf_op jit(solution)/shard_map/scatter-add | solution.py:221
  362.1 1.7 multiply_reduce_fusion.4
  363.8 1.4 pad_maximum_fusion.21
  365.1 65.7 %psum.38 = f32[2]{0:T(128)S(1)} all-reduce(f32[2]{0:T(128)S(1)} %pad_maximum_fusion.21), channel_id=1, replica_groups=mesh['chord'=8,'span'=16] {'chord','span'}, use_global_device_ids=true, to_apply=%region_119.120 | all-reduce | flops 2 | bytes 16 | tf_op jit(solution)/shard_map/psum | solution.py:239
  431.4 2.0 multiply_reduce_fusion.2
  433.5 62.6 %psum.39 = f32[]{:T(128)} all-reduce(f32[]{:T(128)} %get-tuple-element.192), channel_id=1, replica_groups=mesh['chord'=8,'span'=16] {'chord','span'}, use_global_device_ids=true, to_apply=%region_121.122 | all-reduce | flops 1 | bytes 8 | tf_op jit(solution)/shard_map/psum | solution.py:243
  (688 shorter events, 71.3 us)
Async XLA Ops:
  0.6 83.0 %copy-start.226 = (f32[6]{0:T(128)S(1)}, f32[6]{0:T(128)}, u32[]{:S(2)}) copy-start(f32[6]{0:T(128)} %constant.306.clone) | copy-start | bytes 76
  0.6 83.0 %copy-start.221 = (f32[6]{0:T(128)S(1)}, f32[6]{0:T(128)}, u32[]{:S(2)}) copy-start(f32[6]{0:T(128)} %constant.304.clone) | copy-start | bytes 76
  0.7 83.0 %copy-start.223 = (f32[6]{0:T(128)S(1)}, f32[6]{0:T(128)}, u32[]{:S(2)}) copy-start(f32[6]{0:T(128)} %constant.305.clone) | copy-start | bytes 76
  0.7 83.0 %copy-start = (f32[6,12,8,128]{3,2,1,0:T(8,128)S(1)}, f32[6,12,8,128]{3,2,1,0:T(8,128)}, u32[]{:S(2)}) copy-start(f32[6,12,8,128]{3,2,1,0:T(8,128)} %param.41) | copy-start | bytes 884740
  0.7 82.9 %copy-start.14 = (f32[3,12,8,128]{3,2,1,0:T(8,128)S(1)}, f32[3,12,8,128]{3,2,1,0:T(8,128)}, u32[]{:S(2)}) copy-start(f32[3,12,8,128]{3,2,1,0:T(8,128)} %param.42) | copy-start | bytes 442372
  0.7 78.4 %copy-start.1 = (f32[6,12,8,128]{3,2,1,0:T(8,128)S(1)}, f32[6,12,8,128]{3,2,1,0:T(8,128)}, u32[]{:S(2)}) copy-start(f32[6,12,8,128]{3,2,1,0:T(8,128)} %param.45) | copy-start | bytes 884740
  0.7 82.8 %copy-start.225 = (s32[8,128]{1,0:T(8,128)S(1)}, s32[8,128]{1,0:T(8,128)}, u32[]{:S(2)}) copy-start(s32[8,128]{1,0:T(8,128)} %param.44) | copy-start | bytes 12292
  2.8 90.9 %collective-permute-start = (f32[9,12,2,128]{3,2,1,0:T(2,128)S(1)}, f32[9,12,2,128]{3,2,1,0:T(2,128)S(1)}, u32[]{:S(2)}, u32[]{:S(2)}) collective-permute-start(f32[9,12,2,128]{3,2,1,0:T(2,128)S(1)} %get-tuple-element.520), channel_id=1, source_target_pairs={{16,0},{32,16},{48,32},{64,48},{80,64},{96,80},{112,96},{0,112},{1... | collective-permute-start | bytes 331784 | tf_op jit(solution)/shard_map/ppermute | solution.py:36
  11.4 82.3 %collective-permute-start.1 = (f32[9,12,2,128]{3,2,1,0:T(2,128)S(1)}, f32[9,12,2,128]{3,2,1,0:T(2,128)S(1)}, u32[]{:S(2)}, u32[]{:S(2)}) collective-permute-start(f32[9,12,2,128]{3,2,1,0:T(2,128)S(1)} %get-tuple-element.519), channel_id=1, source_target_pairs={{0,16},{16,32},{32,48},{48,64},{64,80},{80,96},{96,112},{112,0},{1... | collective-permute-start | bytes 331784 | tf_op jit(solution)/shard_map/ppermute | solution.py:34
  79.8 34.5 %collective-permute-start.7 = (f32[6,12,8,1]{3,2,1,0:T(8,128)}, f32[6,12,8,1]{3,2,1,0:T(8,128)}, u32[]{:S(2)}, u32[]{:S(2)}) collective-permute-start(f32[6,12,8,1]{3,2,1,0:T(8,128)} %bitcast.1725), channel_id=1, source_target_pairs={{1,0},{2,1},{3,2},{4,3},{5,4},{6,5},{7,6},{8,7},{9,8},{10,9},{11,1... | collective-permute-start | bytes 6920 | tf_op jit(solution)/shard_map/ppermute | solution.py:24
  81.7 12.0 %collective-permute-start.2 = (f32[6,12,1,128]{3,2,1,0:T(1,128)S(1)}, f32[6,12,1,128]{3,2,1,0:T(1,128)S(1)}, u32[]{:S(2)}, u32[]{:S(2)}) collective-permute-start(f32[6,12,1,128]{3,2,1,0:T(1,128)S(1)} %slice.1056), channel_id=1, source_target_pairs={{16,0},{32,16},{48,32},{64,48},{80,64},{96,80},{112,96},{0,112},{1... | collective-permute-start | bytes 110600 | tf_op jit(solution)/shard_map/ppermute | solution.py:24
  101.8 5.8 %collective-permute-start.5 = (f32[9,12,12,2]{2,3,1,0:T(2,128)S(1)}, f32[9,12,12,2]{2,3,1,0:T(2,128)}, u32[]{:S(2)}, u32[]{:S(2)}) collective-permute-start(f32[9,12,12,2]{2,3,1,0:T(2,128)S(1)} %copy.105), channel_id=1, source_target_pairs={{1,0},{2,1},{3,2},{4,3},{5,4},{6,5},{7,6},{8,7},{9,8},{10,9},{11,1... | collective-permute-start | bytes 31112 | tf_op jit(solution)/shard_map/ppermute | solution.py:36
  106.1 5.7 %collective-permute-start.6 = (f32[9,12,12,2]{2,3,1,0:T(2,128)}, f32[9,12,12,2]{2,3,1,0:T(2,128)}, u32[]{:S(2)}, u32[]{:S(2)}) collective-permute-start(f32[9,12,12,2]{2,3,1,0:T(2,128)} %copy.106), channel_id=1, source_target_pairs={{0,1},{1,2},{2,3},{3,4},{4,5},{5,6},{6,7},{7,8},{8,9},{9,10},{10,1... | collective-permute-start | bytes 31112 | tf_op jit(solution)/shard_map/ppermute | solution.py:34
  117.8 28.3 %copy-start.2 = (f32[6,12,8,128]{3,2,1,0:T(8,128)}, f32[6,12,8,128]{3,2,1,0:T(8,128)S(1)}, u32[]{:S(2)}) copy-start(f32[6,12,8,128]{3,2,1,0:T(8,128)S(1)} %get-tuple-element.331) | copy-start | bytes 884740
  117.8 28.3 %copy-start.4 = (f32[6,12,8,128]{3,2,1,0:T(8,128)}, f32[6,12,8,128]{3,2,1,0:T(8,128)S(1)}, u32[]{:S(2)}) copy-start(f32[6,12,8,128]{3,2,1,0:T(8,128)S(1)} %get-tuple-element.332) | copy-start | bytes 884740
  117.8 31.3 %copy-start.28 = (f32[6,12,8,128]{3,2,1,0:T(8,128)}, f32[6,12,8,128]{3,2,1,0:T(8,128)S(1)}, u32[]{:S(2)}) copy-start(f32[6,12,8,128]{3,2,1,0:T(8,128)S(1)} %get-tuple-element.333) | copy-start | bytes 884740
  117.8 32.7 %copy-start.31 = (f32[6,12,8,128]{3,2,1,0:T(8,128)}, f32[6,12,8,128]{3,2,1,0:T(8,128)S(1)}, u32[]{:S(2)}) copy-start(f32[6,12,8,128]{3,2,1,0:T(8,128)S(1)} %get-tuple-element.335) | copy-start | bytes 884740
  117.9 28.3 %copy-start.110 = (f32[12,8,128]{2,1,0:T(8,128)}, f32[12,8,128]{2,1,0:T(8,128)S(1)}, u32[]{:S(2)}) copy-start(f32[12,8,128]{2,1,0:T(8,128)S(1)} %slice_bitcast_fusion.2) | copy-start | bytes 147460
  117.9 29.3 %copy-start.21 = (f32[6,12,8,128]{3,2,1,0:T(8,128)}, f32[6,12,8,128]{3,2,1,0:T(8,128)S(1)}, u32[]{:S(2)}) copy-start(f32[6,12,8,128]{3,2,1,0:T(8,128)S(1)} %add_multiply_fusion.6) | copy-start | bytes 884740
  117.9 28.2 %copy-start.112 = (f32[12,8,128]{2,1,0:T(8,128)}, f32[12,8,128]{2,1,0:T(8,128)S(1)}, u32[]{:S(2)}) copy-start(f32[12,8,128]{2,1,0:T(8,128)S(1)} %slice_bitcast_fusion.3) | copy-start | bytes 147460
  118.2 23.3 %copy-start.46 = (f32[3,12,8,128]{3,2,1,0:T(8,128)}, f32[3,12,8,128]{3,2,1,0:T(8,128)S(1)}, u32[]{:S(2)}) copy-start(f32[3,12,8,128]{3,2,1,0:T(8,128)S(1)} %get-tuple-element.457) | copy-start | bytes 442372
  118.3 24.1 %copy-start.86 = (f32[12,8,128]{2,1,0:T(8,128)}, f32[12,8,128]{2,1,0:T(8,128)S(1)}, u32[]{:S(2)}) copy-start(f32[12,8,128]{2,1,0:T(8,128)S(1)} %get-tuple-element.456) | copy-start | bytes 147460
  118.3 32.5 %copy-start.44 = (f32[3,12,8,128]{3,2,1,0:T(8,128)}, f32[3,12,8,128]{3,2,1,0:T(8,128)S(1)}, u32[]{:S(2)}) copy-start(f32[3,12,8,128]{3,2,1,0:T(8,128)S(1)} %get-tuple-element.394) | copy-start | bytes 442372
  119.2 23.2 %copy-start.118 = (f32[1,12,8,128]{3,2,1,0:T(8,128)}, f32[1,12,8,128]{3,2,1,0:T(8,128)S(1)}, u32[]{:S(2)}) copy-start(f32[1,12,8,128]{3,2,1,0:T(8,128)S(1)} %get-tuple-element.646) | copy-start | bytes 147460
  119.2 32.5 %copy-start.15 = (f32[1,12,8,128]{3,2,1,0:T(8,128)}, f32[1,12,8,128]{3,2,1,0:T(8,128)S(1)}, u32[]{:S(2)}) copy-start(f32[1,12,8,128]{3,2,1,0:T(8,128)S(1)} %get-tuple-element.648) | copy-start | bytes 147460
  119.2 32.5 %copy-start.59 = (f32[1,12,8,128]{3,2,1,0:T(8,128)}, f32[1,12,8,128]{3,2,1,0:T(8,128)S(1)}, u32[]{:S(2)}) copy-start(f32[1,12,8,128]{3,2,1,0:T(8,128)S(1)} %get-tuple-element.645) | copy-start | bytes 147460
  120.0 24.0 %copy-start.57 = (f32[1,12,8,128]{3,2,1,0:T(8,128)}, f32[1,12,8,128]{3,2,1,0:T(8,128)S(1)}, u32[]{:S(2)}) copy-start(f32[1,12,8,128]{3,2,1,0:T(8,128)S(1)} %get-tuple-element.347) | copy-start | bytes 147460
  123.6 22.5 %copy-start.50 = (f32[3,12,8,128]{3,2,1,0:T(8,128)}, f32[3,12,8,128]{3,2,1,0:T(8,128)S(1)}, u32[]{:S(2)}) copy-start(f32[3,12,8,128]{3,2,1,0:T(8,128)S(1)} %get-tuple-element.328) | copy-start | bytes 442372
  123.7 23.5 %copy-start.120 = (f32[12,8,128]{2,1,0:T(8,128)}, f32[12,8,128]{2,1,0:T(8,128)S(1)}, u32[]{:S(2)}) copy-start(f32[12,8,128]{2,1,0:T(8,128)S(1)} %get-tuple-element.127) | copy-start | bytes 147460
  125.2 21.9 %copy-start.69 = (f32[12,8,128]{2,1,0:T(8,128)}, f32[12,8,128]{2,1,0:T(8,128)S(1)}, u32[]{:S(2)}) copy-start(f32[12,8,128]{2,1,0:T(8,128)S(1)} %get-tuple-element.157) | copy-start | bytes 147460
  131.0 23.8 %copy-start.30 = (f32[6,12,8,128]{3,2,1,0:T(8,128)}, f32[6,12,8,128]{3,2,1,0:T(8,128)S(1)}, u32[]{:S(2)}) copy-start(f32[6,12,8,128]{3,2,1,0:T(8,128)S(1)} %get-tuple-element.352) | copy-start | bytes 884740
  132.3 22.5 %copy-start.35 = (f32[6,12,8,128]{3,2,1,0:T(8,128)}, f32[6,12,8,128]{3,2,1,0:T(8,128)S(1)}, u32[]{:S(2)}) copy-start(f32[6,12,8,128]{3,2,1,0:T(8,128)S(1)} %get-tuple-element.368) | copy-start | bytes 884740
  153.7 10.0 %collective-permute-start.8 = (f32[6,12,8,1]{3,2,1,0:T(8,128)S(1)}, f32[6,12,8,1]{3,2,1,0:T(8,128)S(1)}, u32[]{:S(2)}, u32[]{:S(2)}) collective-permute-start(f32[6,12,8,1]{3,2,1,0:T(8,128)S(1)} %slice.1091), channel_id=1, source_target_pairs={{1,0},{2,1},{3,2},{4,3},{5,4},{6,5},{7,6},{8,7},{9,8},{10,9},{11,1... | collective-permute-start | bytes 6920 | tf_op jit(solution)/shard_map/ppermute | solution.py:24
  157.2 14.1 %collective-permute-start.9 = (f32[6,12,8,2]{3,2,1,0:T(8,128)}, f32[6,12,8,2]{3,2,1,0:T(8,128)}, u32[]{:S(2)}, u32[]{:S(2)}) collective-permute-start(f32[6,12,8,2]{3,2,1,0:T(8,128)} %slice.1093), channel_id=1, source_target_pairs={{15,0},{0,1},{1,2},{2,3},{3,4},{4,5},{5,6},{6,7},{7,8},{8,9},{9,10... | collective-permute-start | bytes 13832 | tf_op jit(solution)/shard_map/ppermute | solution.py:24
  157.8 20.6 %collective-permute-start.4 = (f32[6,12,2,128]{3,2,1,0:T(2,128)}, f32[6,12,2,128]{3,2,1,0:T(2,128)}, u32[]{:S(2)}, u32[]{:S(2)}) collective-permute-start(f32[6,12,2,128]{3,2,1,0:T(2,128)} %pad_add_fusion.37), channel_id=1, source_target_pairs={{112,0},{0,16},{16,32},{32,48},{48,64},{64,80},{80,96},{96,112},{1... | collective-permute-start | bytes 221192 | tf_op jit(solution)/shard_map/ppermute | solution.py:24
  157.8 17.1 %collective-permute-start.3 = (f32[6,12,1,128]{3,2,1,0:T(1,128)}, f32[6,12,1,128]{3,2,1,0:T(1,128)}, u32[]{:S(2)}, u32[]{:S(2)}) collective-permute-start(f32[6,12,1,128]{3,2,1,0:T(1,128)} %pad_add_fusion.39), channel_id=1, source_target_pairs={{16,0},{32,16},{48,32},{64,48},{80,64},{96,80},{112,96},{0,112},{1... | collective-permute-start | bytes 110600 | tf_op jit(solution)/shard_map/ppermute | solution.py:24
  178.4 136.2 %copy-start.41 = (f32[12,8,128]{2,1,0:T(8,128)S(1)}, f32[12,8,128]{2,1,0:T(8,128)}, u32[]{:S(2)}) copy-start(f32[12,8,128]{2,1,0:T(8,128)} %copy-done.40) | copy-start | bytes 147460
  178.4 136.2 %copy-start.82 = (f32[12,8,128]{2,1,0:T(8,128)S(1)}, f32[12,8,128]{2,1,0:T(8,128)}, u32[]{:S(2)}) copy-start(f32[12,8,128]{2,1,0:T(8,128)} %copy-done.81) | copy-start | bytes 147460
  178.4 136.2 %copy-start.162 = (f32[12,8,128]{2,1,0:T(8,128)S(1)}, f32[12,8,128]{2,1,0:T(8,128)}, u32[]{:S(2)}) copy-start(f32[12,8,128]{2,1,0:T(8,128)} %param.43) | copy-start | bytes 147460
  182.0 133.8 %copy-start.27 = (f32[13,8,128]{2,1,0:T(8,128)S(1)}, f32[13,8,128]{2,1,0:T(8,128)}, u32[]{:S(2)}) copy-start(f32[13,8,128]{2,1,0:T(8,128)} %copy-done.26) | copy-start | bytes 159748
  182.0 133.8 %copy-start.155 = (f32[13,8,128]{2,1,0:T(8,128)S(1)}, f32[13,8,128]{2,1,0:T(8,128)}, u32[]{:S(2)}) copy-start(f32[13,8,128]{2,1,0:T(8,128)} %copy-done.154) | copy-start | bytes 159748
  314.4 25.6 %copy-start.19 = (f32[6,12,8,128]{3,2,1,0:T(8,128)}, f32[6,12,8,128]{3,2,1,0:T(8,128)S(1)}, u32[]{:S(2)}) copy-start(f32[6,12,8,128]{3,2,1,0:T(8,128)S(1)} %broadcast_divide_fusion.1) | copy-start | bytes 884740
  315.9 9.5 %collective-permute-start.13 = (f32[6,12,8,1]{3,2,1,0:T(8,128)S(1)}, f32[6,12,8,1]{3,2,1,0:T(8,128)S(1)}, u32[]{:S(2)}, u32[]{:S(2)}) collective-permute-start(f32[6,12,8,1]{3,2,1,0:T(8,128)S(1)} %bitcast.1735), channel_id=1, source_target_pairs={{1,0},{2,1},{3,2},{4,3},{5,4},{6,5},{7,6},{8,7},{9,8},{10,9},{11,1... | collective-permute-start | bytes 6920 | tf_op jit(solution)/shard_map/ppermute | solution.py:24
  316.9 8.5 %collective-permute-start.10 = (f32[6,12,1,128]{3,2,1,0:T(1,128)S(1)}, f32[6,12,1,128]{3,2,1,0:T(1,128)S(1)}, u32[]{:S(2)}, u32[]{:S(2)}) collective-permute-start(f32[6,12,1,128]{3,2,1,0:T(1,128)S(1)} %slice.1122), channel_id=1, source_target_pairs={{16,0},{32,16},{48,32},{64,48},{80,64},{96,80},{112,96},{0,112},{1... | collective-permute-start | bytes 110600 | tf_op jit(solution)/shard_map/ppermute | solution.py:24
  345.8 8.6 %collective-permute-start.14 = (f32[6,12,8,1]{3,2,1,0:T(8,128)S(1)}, f32[6,12,8,1]{3,2,1,0:T(8,128)S(1)}, u32[]{:S(2)}, u32[]{:S(2)}) collective-permute-start(f32[6,12,8,1]{3,2,1,0:T(8,128)S(1)} %slice.1128), channel_id=1, source_target_pairs={{1,0},{2,1},{3,2},{4,3},{5,4},{6,5},{7,6},{8,7},{9,8},{10,9},{11,1... | collective-permute-start | bytes 6920 | tf_op jit(solution)/shard_map/ppermute | solution.py:24
  349.1 10.7 %collective-permute-start.15 = (f32[6,12,8,2]{3,2,1,0:T(8,128)}, f32[6,12,8,2]{3,2,1,0:T(8,128)}, u32[]{:S(2)}, u32[]{:S(2)}) collective-permute-start(f32[6,12,8,2]{3,2,1,0:T(8,128)} %slice.1130), channel_id=1, source_target_pairs={{15,0},{0,1},{1,2},{2,3},{3,4},{4,5},{5,6},{6,7},{7,8},{8,9},{9,10... | collective-permute-start | bytes 13832 | tf_op jit(solution)/shard_map/ppermute | solution.py:24
  349.1 12.8 %collective-permute-start.12 = (f32[6,12,2,128]{3,2,1,0:T(2,128)}, f32[6,12,2,128]{3,2,1,0:T(2,128)S(1)}, u32[]{:S(2)}, u32[]{:S(2)}) collective-permute-start(f32[6,12,2,128]{3,2,1,0:T(2,128)} %pad_add_fusion.36), channel_id=1, source_target_pairs={{112,0},{0,16},{16,32},{32,48},{48,64},{64,80},{80,96},{96,112},{1... | collective-permute-start | bytes 221192 | tf_op jit(solution)/shard_map/ppermute | solution.py:24
  349.2 12.5 %collective-permute-start.11 = (f32[6,12,1,128]{3,2,1,0:T(1,128)S(1)}, f32[6,12,1,128]{3,2,1,0:T(1,128)S(1)}, u32[]{:S(2)}, u32[]{:S(2)}) collective-permute-start(f32[6,12,1,128]{3,2,1,0:T(1,128)S(1)} %pad_add_fusion.38), channel_id=1, source_target_pairs={{16,0},{32,16},{48,32},{64,48},{80,64},{96,80},{112,96},{0,112},{1... | collective-permute-start | bytes 110600 | tf_op jit(solution)/shard_map/ppermute | solution.py:24
  (197 other events, 640.4 us)
where the time goes:
time: 509 us; the launch traced here: 499 us
  blocking collectives  326 us (64%)
  other arithmetic  95.2 us (19%)
  local copies, waits for them, and re-layouts  42.3 us (8%)
  starting transfers between devices  28.3 us (6%)
  between operations  7.21 us (1%)
    psum x2, blocking collectives, orthogonal(): coefficients = lax.psum(partial_value, ('chord', 'span')) / entries  132 us
    psum x2, blocking collectives, orthogonal(): lax.psum(jnp.sum(mapped * mapped), ('chord', 'span')) / entries + NORM_EPS  127 us
    psum x1, blocking collectives, on_device(): lax.psum(jnp.sum(cost_gradient * cost_gradient), ('chord', 'span'))  67 us
    ppermute x12, starting transfers between devices, passed_along(): return lax.ppermute(block, axis, route)  19.4 us
    scatter-add x2, local copies, waits for them, and re-layouts, span_return(): own_part = own_part.at[:, :, :, cells_along - 1:].add(from_above)  12.2 us
    unnamed x461, local copies, waits for them, and re-layouts  11.6 us
  transfers between devices with their start and end apart: 16, of which 0 were waited for; matrix products, arithmetic and copies ran while one was open for 12% of the time, Pallas kernels for 0%

commit v1 on v0

v1 whole, which is shorter than its diff:
```python
import functools

import jax
import jax.numpy as jnp
from jax import lax
from jax.experimental import pallas as pl
from jax.experimental.pallas import tpu as pltpu
from jax.sharding import PartitionSpec as P

HEAT_RATIO = 1.4
GAMMA_LESS = 0.4
VISCOSITY = 0.2
HEAT_FACTOR = 1.4 / (0.4 * 0.72)
CB_ONE = 0.1355
CW_ONE = 3.239
CV_CUBE = 7.1 * 7.1 * 7.1
TURB_SIGMA = 2.0 / 3.0
LIMIT_EPS = 0.01
NORM_EPS = 1e-06
FREESTREAM = (1.0, 0.2, 0.0, 0.05, 2.5, 0.1)
SLIP_SIGNS = (1.0, 1.0, 1.0, -1.0, 1.0, 1.0)
WALL_SIGNS = (1.0, -1.0, -1.0, -1.0, 1.0, -1.0)

HEAT_E = GAMMA_LESS * HEAT_FACTOR
HEAT_K = 1.0 - GAMMA_LESS * HEAT_FACTOR
CUBE_SHIFT = VISCOSITY * VISCOSITY * VISCOSITY * CV_CUBE

LAYERS, CX, CY = 12, 8, 128
ROWS = LAYERS * CX

COL_STEP, COL_OWN, COL_ROWS = 8, 32, 160
CHORD_STEP, CHORD_OWN, CHORD_ROWS = 12, 40, 176
SPAN_STEP, SPAN_OWN, SPAN_ROWS = 1, 16, 160

FL, FR, FN, FD, FM, FS, FQ, FK, FE, FRH, FTH = 0, 7, 14, 17, 23, 28, 29, 30, 31, 36, 37
FACE_COUNT = 38
GL, GR, PU, PH, TL, TR, RB = 0, 6, 12, 15, 16, 17, 18
RESULT_COUNT = 19


def blocks(first, last, size, body):
    def step(index, carry):
        body(pl.multiple_of(first + index * size, 8))
        return carry

    lax.fori_loop(0, (last - first) // size, step, 0)


def dot3(a, b):
    return a[0] * b[0] + a[1] * b[1] + a[2] * b[2]


def primitives(state):
    inverse = 1.0 / state[0]
    velocity = [state[1 + j] * inverse for j in range(3)]
    return inverse, velocity, state[5] * inverse, state[4] * inverse


def slopes_stage(step, first, last, size, window, halves, pulls, prims):
    def body(row):
        here_all = []
        for k in range(6):
            before = window[k, pl.ds(row - step, size), :]
            here = window[k, pl.ds(row, size), :]
            after = window[k, pl.ds(row + step, size), :]
            p = here - before
            q = after - here
            pp = p * p + LIMIT_EPS
            qq = q * q + LIMIT_EPS
            inverse = 1.0 / (pp + qq)
            slope = (qq * p + pp * q) * inverse
            half_inverse = 0.5 * inverse
            a = (qq + 2.0 * p * (q - slope)) * half_inverse
            b = (pp + 2.0 * q * (p - slope)) * half_inverse
            rows = pl.ds(row, size)
            halves[k, rows, :] = here + 0.5 * slope
            halves[6 + k, rows, :] = here - 0.5 * slope
            pulls[k, rows, :] = a
            pulls[6 + k, rows, :] = b
            pulls[12 + k, rows, :] = a - b
            here_all.append(here)
        inverse, velocity, turbulence, specific = primitives(here_all)
        rows = pl.ds(row, size)
        prims[0, rows, :] = inverse
        for j in range(3):
            prims[1 + j, rows, :] = velocity[j]
        prims[4, rows, :] = turbulence
        prims[5, rows, :] = specific

    blocks(first, last, size, body)


def side_coefficients(state, normal):
    inverse, velocity, turbulence, specific = primitives(state)
    kinetic = 0.5 * dot3(velocity, velocity)
    pressure_ratio = GAMMA_LESS * (specific - kinetic)
    return velocity + [kinetic, specific + pressure_ratio, turbulence, dot3(velocity, normal)]


def faces_stage(step, direction, first, last, size, window, offsets, halves, prims, faces):
    def body(row):
        here = pl.ds(row, size)
        after = pl.ds(row + step, size)
        spacing = [offsets[j, after, :] - offsets[j, here, :] for j in range(3)]
        spacing[direction] = spacing[direction] + 1.0
        weight = lax.rsqrt(dot3(spacing, spacing))
        normal = [spacing[j] * weight for j in range(3)]
        left = [halves[k, here, :] for k in range(6)]
        right = [halves[6 + k, after, :] for k in range(6)]
        for slot, value in enumerate(side_coefficients(left, normal)):
            faces[FL + slot, here, :] = value
        for slot, value in enumerate(side_coefficients(right, normal)):
            faces[FR + slot, here, :] = value
        for j in range(3):
            faces[FN + j, here, :] = normal[j]
        for k in range(6):
            faces[FD + k, here, :] = left[k] - right[k]
        middle = [0.5 * (left[k] + right[k]) for k in range(5)] + [left[5]]
        inverse, velocity, unused, specific = primitives(middle)
        kinetic = 0.5 * dot3(velocity, velocity)
        speed = dot3(velocity, normal)
        sound_square = HEAT_RATIO * GAMMA_LESS * (specific - kinetic)
        sound_inverse = lax.rsqrt(sound_square)
        size_speed = jnp.abs(speed)
        sign = jnp.where(speed > 0.0, 1.0, jnp.where(speed < 0.0, -1.0, 0.0))
        half_inverse = 0.5 * inverse
        factor = 0.5 * HEAT_RATIO * GAMMA_LESS * sound_inverse
        faces[FS, here, :] = size_speed + sound_square * sound_inverse
        faces[FM, here, :] = half_inverse * (factor * (2.0 * kinetic - specific) - size_speed)
        for j in range(3):
            faces[FM + 1 + j, here, :] = half_inverse * (sign * normal[j] - factor * velocity[j])
        faces[FM + 4, here, :] = half_inverse * factor
        velocity_l = [prims[1 + j, here, :] for j in range(3)]
        velocity_r = [prims[1 + j, after, :] for j in range(3)]
        jump = [velocity_r[j] - velocity_l[j] for j in range(3)]
        kinetic_jump = 0.5 * (dot3(velocity_r, velocity_r) - dot3(velocity_l, velocity_l))
        heat_jump = HEAT_E * (prims[5, after, :] - prims[5, here, :]) + HEAT_K * kinetic_jump
        turbulence_l, turbulence_r = prims[4, here, :], prims[4, after, :]
        half_density = 0.25 * (window[0, here, :] + window[0, after, :])
        half_turbulence = 0.25 * (turbulence_l + turbulence_r)
        mixed = 4.0 * half_density * half_turbulence
        cube = mixed * mixed * mixed
        ratio = cube / (cube + CUBE_SHIFT)
        twice = 2.0 * weight
        pull = -twice * ratio * (4.0 - 3.0 * ratio)
        faces[FQ, here, :] = twice * (VISCOSITY + mixed * ratio)
        faces[FK, here, :] = (VISCOSITY + mixed) * (twice / TURB_SIGMA)
        for j in range(3):
            faces[FE + j, here, :] = pull * jump[j]
        faces[FE + 3, here, :] = pull * heat_jump
        faces[FE + 4, here, :] = -(twice / TURB_SIGMA) * (turbulence_r - turbulence_l)
        faces[FRH, here, :] = half_density
        faces[FTH, here, :] = half_turbulence

    blocks(first, last, size, body)


def side_pullback(faces, here, base, normal, wave, shared, g):
    velocity = [faces[base + j, here, :] for j in range(3)]
    kinetic = faces[base + 3, here, :]
    enthalpy = faces[base + 4, here, :]
    turbulence = faces[base + 5, here, :]
    speed = faces[base + 6, here, :]
    total = g[0] + dot3(velocity, g[1:4]) + enthalpy * g[4] + turbulence * g[5]
    pressure = GAMMA_LESS * (shared + speed * g[4])
    carried = speed + wave
    result = [carried * g[0] - total * speed + pressure * kinetic]
    for j in range(3):
        result.append(carried * g[1 + j] + total * normal[j] - pressure * velocity[j])
    result.append(carried * g[4] + pressure)
    result.append(carried * g[5])
    return result


def pull_stage(step, first, last, size, vector, faces, results):
    def body(row):
        here = pl.ds(row, size)
        after = pl.ds(row + step, size)
        g = [vector[k, here, :] - vector[k, after, :] for k in range(6)]
        normal = [faces[FN + j, here, :] for j in range(3)]
        wave = faces[FS, here, :]
        shared = dot3(normal, g[1:4])
        left = side_pullback(faces, here, FL, normal, wave, shared, g)
        right = side_pullback(faces, here, FR, normal, -wave, shared, g)
        wave_bar = faces[FD, here, :] * g[0]
        for k in range(1, 6):
            wave_bar = wave_bar + faces[FD + k, here, :] * g[k]
        for k in range(6):
            if k < 5:
                middle = wave_bar * faces[FM + k, here, :]
                results[GL + k, here, :] = left[k] + middle
                results[GR + k, here, :] = right[k] + middle
            else:
                results[GL + k, here, :] = left[k]
                results[GR + k, here, :] = right[k]
        viscous = faces[FQ, here, :]
        mixed_bar = faces[FE, here, :] * g[1]
        for k in range(1, 5):
            mixed_bar = mixed_bar + faces[FE + k, here, :] * g[1 + k]
        for j in range(3):
            results[PU + j, here, :] = viscous * g[1 + j]
        results[PH, here, :] = viscous * g[4]
        diffused = faces[FK, here, :] * g[5]
        shift = faces[FRH, here, :] * mixed_bar
        results[TL, here, :] = shift + diffused
        results[TR, here, :] = shift - diffused
        results[RB, here, :] = faces[FTH, here, :] * mixed_bar

    blocks(first, last, size, body)


def cells_stage(step, first, last, size, pulls, prims, results, store, extra=None):
    def body(row):
        here = pl.ds(row, size)
        before = pl.ds(row - step, size)
        after = pl.ds(row + step, size)
        twice = pl.ds(row - 2 * step, size)
        outcome = []
        for k in range(6):
            gl, gr = results[GL + k, here, :], results[GR + k, before, :]
            value = gl + gr + pulls[12 + k, here, :] * (gl - gr)
            value = value + pulls[6 + k, before, :] * (
                results[GL + k, before, :] - results[GR + k, twice, :]
            )
            value = value - pulls[k, after, :] * (
                results[GL + k, after, :] - results[GR + k, here, :]
            )
            outcome.append(value)
        velocity_bar = [results[PU + j, here, :] - results[PU + j, before, :] for j in range(3)]
        heat_bar = results[PH, here, :] - results[PH, before, :]
        turbulence_bar = results[TL, here, :] + results[TR, before, :]
        density_bar = results[RB, here, :] + results[RB, before, :]
        inverse = prims[0, here, :]
        velocity = [prims[1 + j, here, :] for j in range(3)]
        if extra is not None:
            velocity_bar, turbulence_bar, density_bar = extra(
                row, velocity, velocity_bar, turbulence_bar, density_bar
            )
        kinetic_bar = HEAT_K * heat_bar
        energy_bar = HEAT_E * heat_bar
        velocity_bar = [velocity_bar[j] + kinetic_bar * velocity[j] for j in range(3)]
        scaled = (
            dot3(velocity_bar, velocity)
            + energy_bar * prims[5, here, :]
            + turbulence_bar * prims[4, here, :]
        )
        outcome[0] = outcome[0] + density_bar - scaled * inverse
        for j in range(3):
            outcome[1 + j] = outcome[1 + j] + velocity_bar[j] * inverse
        outcome[4] = outcome[4] + energy_bar * inverse
        outcome[5] = outcome[5] + turbulence_bar * inverse
        store(row, outcome)

    blocks(first, last, size, body)


def kernel(
    chord_count, span_count, entries,
    flow, offset, wall, codes, cost, basis, hessenberg,
    wu, wd, wv, cu, cd, cv, su, sd, sv, halves,
    col_pulls, col_prims, col_faces, chord_pulls, chord_prims, chord_faces,
    span_pulls, span_prims, span_faces, results, source, signs, col_out, chord_out, span_out,
    mapped, span_sums, chord_sums, send_sem, recv_sem, sum_send, sum_recv,
):
    chord_id, span_id = lax.axis_index("chord"), lax.axis_index("span")

    def chord_at(distance):
        return lax.rem(chord_id + (distance + chord_count), chord_count)

    def span_at(distance):
        return lax.rem(span_id + (distance + span_count), span_count)

    barrier = pltpu.get_barrier_semaphore()
    for d in range(1, chord_count):
        pl.semaphore_signal(barrier, inc=1, device_id=(chord_at(d), span_id), device_id_type=pl.DeviceIdType.MESH)
    for d in range(1, span_count):
        pl.semaphore_signal(barrier, inc=1, device_id=(chord_id, span_at(d)), device_id_type=pl.DeviceIdType.MESH)

    def to_chord_rows(source_ref, target, count):
        def body(k, carry):
            for cell in range(CX):
                base = CHORD_OWN + cell * LAYERS
                target[k, pl.ds(base, 8), :] = source_ref[k, pl.ds(COL_OWN + cell, 8, stride=CX), :]
                target[k, pl.ds(base + 8, 4), :] = source_ref[
                    k, pl.ds(COL_OWN + 8 * CX + cell, 4, stride=CX), :
                ]
            return carry

        lax.fori_loop(0, count, body, 0)

    def to_span_rows(source_ref, target, count):
        def body(k, carry):
            target[k, pl.ds(SPAN_OWN, CY), :] = source_ref[k, pl.ds(COL_OWN, CY), :].T
            return carry

        lax.fori_loop(0, count, body, 0)

    started = []

    def exchange(slot, ref, chordwise, depth):
        if chordwise:
            rows = 40 if depth == 3 else 24
            tail = CHORD_OWN + ROWS - rows
            moves = (
                (tail, CHORD_OWN - rows, (chord_at(1), span_id)),
                (CHORD_OWN, CHORD_OWN + ROWS, (chord_at(-1), span_id)),
            )
        else:
            rows = 8
            moves = (
                (SPAN_OWN + CY - rows, SPAN_OWN - rows, (chord_id, span_at(1))),
                (SPAN_OWN, SPAN_OWN + CY, (chord_id, span_at(-1))),
            )
        copies = []
        for side, (first, landing, target) in enumerate(moves):
            copy = pltpu.make_async_remote_copy(
                src_ref=ref.at[:, pl.ds(first, rows), :],
                dst_ref=ref.at[:, pl.ds(landing, rows), :],
                send_sem=send_sem.at[slot, side],
                recv_sem=recv_sem.at[slot, side],
                device_id=target,
                device_id_type=pl.DeviceIdType.MESH,
            )
            copy.start()
            copies.append(copy)
        started.extend(copies)
        return copies

    def arrive(copies):
        for copy in copies:
            copy.wait_recv()

    own = pl.ds(COL_OWN, ROWS)
    code = codes[...]
    for k in range(6):
        near, far = flow[k, 0:8, :], flow[k, 8:16, :]
        sign = jnp.where(code == 0, SLIP_SIGNS[k], jnp.where(code == 1, WALL_SIGNS[k], 0.0))
        level = jnp.where((code == 0) | (code == 1), 0.0, FREESTREAM[k])
        signs[k] = sign
        wu[k, 0:16, :] = jnp.full((16, CY), FREESTREAM[k], jnp.float32)
        wu[k, 16:24, :] = sign * far + level
        wu[k, 24:32, :] = sign * near + level
        wu[k, own, :] = flow[k]
        wu[k, 128:160, :] = jnp.full((32, CY), FREESTREAM[k], jnp.float32)
        wv[0, k, 0:32, :] = jnp.zeros((32, CY), jnp.float32)
        wv[0, k, own, :] = 0.5 * cost[k]
        wv[0, k, 128:160, :] = jnp.zeros((32, CY), jnp.float32)
        wv[1, k, 0:32, :] = jnp.zeros((32, CY), jnp.float32)
        wv[1, k, 128:160, :] = jnp.zeros((32, CY), jnp.float32)
    for j in range(3):
        near, far, top = offset[j, 0:8, :], offset[j, 8:16, :], offset[j, 88:96, :]
        wd[j, 0:8, :] = far
        wd[j, 8:16, :] = far
        wd[j, 16:24, :] = far
        wd[j, 24:32, :] = near
        wd[j, own, :] = offset[j]
        for layer in range(4):
            wd[j, 128 + 8 * layer : 136 + 8 * layer, :] = top

    to_chord_rows(wu, cu, 6)
    to_span_rows(wu, su, 6)
    to_chord_rows(wd, cd, 3)
    to_span_rows(wd, sd, 3)
    to_chord_rows(wv.at[0], cv.at[0], 6)
    to_span_rows(wv.at[0], sv.at[0], 6)

    pl.semaphore_wait(barrier, chord_count + span_count - 2)
    chord_flow = exchange(0, cu, True, 3)
    span_flow = exchange(1, su, False, 3)
    chord_offset = exchange(2, cd, True, 2)
    span_offset = exchange(3, sd, False, 2)
    chord_vector = exchange(4, cv.at[0], True, 2)
    span_vector = exchange(5, sv.at[0], False, 2)

    def source_body(row):
        here = pl.ds(row, 16)
        cells = pl.ds(row + COL_OWN, 16)
        density = wu[0, cells, :]
        inverse = 1.0 / density
        velocity = [wu[1 + j, cells, :] * inverse for j in range(3)]
        turbulence = wu[5, cells, :] * inverse
        near = 1.0 / wall[here, :]
        square = dot3(velocity, velocity) + 0.01
        root_inverse = lax.rsqrt(square)
        slope = CB_ONE * near
        shear = slope * (square * root_inverse)
        decay = CW_ONE * turbulence * near * near
        source[0, here, :] = -2.0 * turbulence * (shear - decay)
        source[1, here, :] = -2.0 * density * (shear - 2.0 * decay)
        source[2, here, :] = -2.0 * density * turbulence * slope * root_inverse

    blocks(0, ROWS, 16, source_body)

    def column_ready():
        slopes_stage(COL_STEP, 16, 144, 16, wu, halves, col_pulls, col_prims)
        faces_stage(COL_STEP, 2, 24, 136, 16, wu, wd, halves, col_prims, col_faces)
        for k in range(6):
            col_pulls[6 + k, 8:16, :] = jnp.zeros((8, CY), jnp.float32)

    def column_product(vector):
        for slot in range(RESULT_COUNT):
            results[slot, 0:24, :] = jnp.zeros((24, CY), jnp.float32)
        pull_stage(COL_STEP, 24, 136, 16, vector, col_faces, results)

        def ghost_store(row, outcome):
            for k in range(6):
                col_out[k, pl.ds(row, 16), :] = outcome[k]

        def with_source(row, velocity, velocity_bar, turbulence_bar, density_bar):
            here = pl.ds(pl.multiple_of(row - COL_OWN, 8), 16)
            value = vector[5, pl.ds(row, 16), :]
            pulled = source[2, here, :] * value
            return (
                [velocity_bar[j] + pulled * velocity[j] for j in range(3)],
                turbulence_bar + source[1, here, :] * value,
                density_bar + source[0, here, :] * value,
            )

        cells_stage(COL_STEP, 16, 32, 16, col_pulls, col_prims, results, ghost_store)
        cells_stage(COL_STEP, 32, 128, 16, col_pulls, col_prims, results, ghost_store, with_source)
        for k in range(6):
            sign = signs[k]
            col_out[k, 32:40, :] = col_out[k, 32:40, :] + sign * col_out[k, 24:32, :]
            col_out[k, 40:48, :] = col_out[k, 40:48, :] + sign * col_out[k, 16:24, :]

    def span_ready():
        slopes_stage(SPAN_STEP, 8, 152, 16, su, halves, span_pulls, span_prims)
        faces_stage(SPAN_STEP, 1, 8, 152, 16, su, sd, halves, span_prims, span_faces)

    def span_product(vector):
        pull_stage(SPAN_STEP, 8, 152, 16, vector, span_faces, results)

        def store(row, outcome):
            for k in range(6):
                span_out[k, pl.ds(pl.multiple_of(row - SPAN_OWN, 8), 16), :] = outcome[k]

        cells_stage(SPAN_STEP, 16, 144, 16, span_pulls, span_prims, results, store)

    def chord_ready():
        slopes_stage(CHORD_STEP, 16, 160, 16, cu, halves, chord_pulls, chord_prims)
        faces_stage(CHORD_STEP, 0, 16, 160, 16, cu, cd, halves, chord_prims, chord_faces)

    def chord_product(vector):
        pull_stage(CHORD_STEP, 16, 160, 16, vector, chord_faces, results)

        def store(row, outcome):
            for k in range(6):
                chord_out[k, pl.ds(pl.multiple_of(row - CHORD_OWN, 8), 16), :] = outcome[k]

        cells_stage(CHORD_STEP, 40, 136, 16, chord_pulls, chord_prims, results, store)

    def combine(target, halved):
        def body(k, carry):
            turned = span_out[k].T
            for layer in range(LAYERS):
                rows = slice(layer * CX, layer * CX + CX)
                value = turned[rows, :] + col_out[k, COL_OWN + layer * CX : COL_OWN + layer * CX + CX, :]
                value = value + chord_out[k, pl.ds(layer, CX, stride=LAYERS), :]
                mapped[target, k, rows, :] = value
                if halved:
                    wv[1, k, COL_OWN + layer * CX : COL_OWN + layer * CX + CX, :] = 0.5 * value
            return carry

        lax.fori_loop(0, 6, body, 0)

    column_ready()
    column_product(wv.at[0])
    arrive(span_flow + span_offset)
    span_ready()
    arrive(span_vector)
    span_product(sv.at[0])
    arrive(chord_flow + chord_offset)
    chord_ready()
    arrive(chord_vector)
    chord_product(cv.at[0])
    combine(0, True)

    to_chord_rows(wv.at[1], cv.at[1], 6)
    chord_vector = exchange(6, cv.at[1], True, 2)
    to_span_rows(wv.at[1], sv.at[1], 6)
    span_vector = exchange(7, sv.at[1], False, 2)

    def inner(pairs):
        def body(k, sums):
            sums = list(sums)
            for layer in range(LAYERS):
                rows = slice(layer * CX, layer * CX + CX)
                values = [cost[k, rows, :], mapped[0, k, rows, :], mapped[1, k, rows, :]]
                for index, (one, two) in enumerate(pairs):
                    sums[index] = sums[index] + values[one] * values[two]
            return tuple(sums)

        return lax.fori_loop(0, 6, body, tuple(jnp.zeros((CX, CY), jnp.float32) for _ in pairs))

    first_sums = inner(((0, 0), (0, 1), (1, 1)))
    column_product(wv.at[1])
    arrive(span_vector)
    span_product(sv.at[1])
    arrive(chord_vector)
    chord_product(cv.at[1])
    combine(1, False)
    second_sums = inner(((0, 2), (1, 2), (2, 2)))

    row_of = lax.broadcasted_iota(jnp.int32, (8, CY), 0)
    packed = jnp.zeros((8, CY), jnp.float32)
    for index, value in enumerate(first_sums + second_sums):
        packed = jnp.where(row_of == index, jnp.sum(value, axis=0, keepdims=True), packed)

    def total_over(value, buffer, count, me, at, first_slot):
        buffer[me] = value
        copies = []
        for d in range(1, count):
            copy = pltpu.make_async_remote_copy(
                src_ref=buffer.at[me],
                dst_ref=buffer.at[me],
                send_sem=sum_send.at[first_slot + d],
                recv_sem=sum_recv.at[first_slot + d],
                device_id=at(d),
                device_id_type=pl.DeviceIdType.MESH,
            )
            copy.start()
            copies.append(copy)
        started.extend(copies)
        arrive(copies)
        total = buffer[0]
        for index in range(1, count):
            total = total + buffer[index]
        return total

    packed = total_over(packed, span_sums, span_count, span_id, lambda d: (chord_id, span_at(d)), 0)
    packed = total_over(packed, chord_sums, chord_count, chord_id, lambda d: (chord_at(d), span_id), span_count)
    means = jnp.sum(packed, axis=1, keepdims=True) * (1.0 / entries)
    means = jnp.broadcast_to(means, (8, CY))
    cc, cm, mm, cn, mn, nn = [means[index : index + 1, :] for index in range(6)]

    scale = lax.rsqrt(cc + NORM_EPS)
    h11 = cm * scale * scale
    fresh = jnp.maximum(mm - 2.0 * h11 * cm + h11 * h11 * cc, 0.0)
    square = fresh * scale * scale + NORM_EPS
    inverse = lax.rsqrt(square)
    h21 = square * inverse
    gain = scale * inverse
    h12 = gain * scale * (cn - h11 * cm)
    h22 = gain * gain * (mn - h11 * cn - h11 * mm + h11 * h11 * cm)
    along_m = -gain * (h11 + h22)
    along_c = h22 * gain * h11 - h12 * scale
    fresh = (
        gain * gain * nn + along_m * along_m * mm + along_c * along_c * cc
        + 2.0 * (gain * along_m * mn + gain * along_c * cn + along_m * along_c * cm)
    )
    square = jnp.maximum(fresh, 0.0) + NORM_EPS
    inverse = lax.rsqrt(square)
    h32 = square * inverse
    factors = [jnp.broadcast_to(f * inverse, (CX, CY)) for f in (along_c, along_m, gain)]
    entries_out = jnp.zeros((8, CY), jnp.float32)
    for index, value in enumerate((h11, h21, h12, h22, h32)):
        entries_out = jnp.where(row_of == index, value, entries_out)
    hessenberg[...] = entries_out

    def final_body(k, carry):
        for layer in range(LAYERS):
            rows = slice(layer * CX, layer * CX + CX)
            basis[k, rows, :] = (
                factors[0] * cost[k, rows, :]
                + factors[1] * mapped[0, k, rows, :]
                + factors[2] * mapped[1, k, rows, :]
            )
        return carry

    lax.fori_loop(0, 6, final_body, 0)
    for copy in started:
        copy.wait_send()


def on_device(chord_count, span_count, flow_state, displacement, wall_distance, face_codes, cost_gradient):
    entries = float(cost_gradient.size * chord_count * span_count)

    def vmem(*shape):
        return pltpu.VMEM(shape, jnp.float32)

    whole = pl.BlockSpec(memory_space=pltpu.VMEM)
    basis, table = pl.pallas_call(
        functools.partial(kernel, chord_count, span_count, entries),
        out_shape=(
            jax.ShapeDtypeStruct((6, ROWS, CY), jnp.float32),
            jax.ShapeDtypeStruct((8, CY), jnp.float32),
        ),
        in_specs=[whole] * 5,
        out_specs=(whole, whole),
        scratch_shapes=[
            vmem(6, COL_ROWS, CY), vmem(3, COL_ROWS, CY), vmem(2, 6, COL_ROWS, CY),
            vmem(6, CHORD_ROWS, CY), vmem(3, CHORD_ROWS, CY), vmem(2, 6, CHORD_ROWS, CY),
            vmem(6, SPAN_ROWS, CY), vmem(3, SPAN_ROWS, CY), vmem(2, 6, SPAN_ROWS, CY),
            vmem(12, CHORD_ROWS, CY),
            vmem(18, COL_ROWS, CY), vmem(6, COL_ROWS, CY), vmem(FACE_COUNT, COL_ROWS, CY),
            vmem(18, CHORD_ROWS, CY), vmem(6, CHORD_ROWS, CY), vmem(FACE_COUNT, CHORD_ROWS, CY),
            vmem(18, SPAN_ROWS, CY), vmem(6, SPAN_ROWS, CY), vmem(FACE_COUNT, SPAN_ROWS, CY),
            vmem(RESULT_COUNT, CHORD_ROWS, CY), vmem(3, ROWS, CY), vmem(6, CX, CY),
            vmem(6, COL_ROWS, CY), vmem(6, ROWS, CY), vmem(6, CY, CY),
            vmem(2, 6, ROWS, CY), vmem(span_count, 8, CY), vmem(chord_count, 8, CY),
            pltpu.SemaphoreType.DMA((8, 2)), pltpu.SemaphoreType.DMA((8, 2)),
            pltpu.SemaphoreType.DMA((span_count + chord_count,)),
            pltpu.SemaphoreType.DMA((span_count + chord_count,)),
        ],
        compiler_params=pltpu.CompilerParams(
            collective_id=0, has_side_effects=True, vmem_limit_bytes=48 * 1024 * 1024
        ),
        name="arnoldi",
    )(
        flow_state.reshape(6, ROWS, CY),
        displacement.reshape(3, ROWS, CY),
        wall_distance.reshape(ROWS, CY),
        face_codes,
        cost_gradient.reshape(6, ROWS, CY),
    )
    return basis.reshape(cost_gradient.shape), table[:5, 0]


def solution(mesh):
    return jax.shard_map(
        functools.partial(on_device, mesh.shape["chord"], mesh.shape["span"]),
        mesh=mesh,
        in_specs=(
            P(None, None, "chord", "span"),
            P(None, None, "chord", "span"),
            P(None, "chord", "span"),
            P("chord", "span"),
            P(None, None, "chord", "span"),
        ),
        out_specs=(P(None, None, "chord", "span"), P()),
        check_vma=False,
    )
```

time: 509 us -> 41.7 us (0.08); the launches traced: 499 us -> 41.4 us
  blocking collectives: 326 us -> 0 us
  other arithmetic: 95.2 us -> 0 us
  local copies, waits for them, and re-layouts: 42.3 us -> 5.65 us
  Pallas kernels: 0 us -> 35.1 us
  starting transfers between devices: 28.3 us -> 0 us
  between operations: 7.21 us -> 0.65 us
    psum x5 -> x0, blocking collectives: 326 us -> none  [the longest x2 132 us: orthogonal(): coefficients = lax.psum(partial_value, ('chord', 'span')) / entries]
    pallas_call x0 -> x1, Pallas kernels: none -> 35.1 us  [on_device(): pl.pallas_call(functools.partial(kernel, chord_count, span_count, entries...]
    reduce_sum x39 -> x0, other arithmetic: 31 us -> none  [the longest x5 10 us: face_flux(): 0.5 * wave_speed * (right_state - left_state)]
    ppermute x16 -> x0, starting transfers between devices: 28.3 us -> none  [the longest x12 19.4 us: passed_along(): return lax.ppermute(block, axis, route)]
    scatter-add x6 -> x0, local copies, waits for them, and re-layouts: 16.7 us -> none  [the longest x2 12.2 us: span_return(): own_part = own_part.at[:, :, :, cells_along - 1:].add(from_above)]
    neg x27 -> x0, other arithmetic: 14.5 us -> none  [the longest x10 6.22 us: face_flux(): right_cell[:6] - left_cell[:6]]
    mul x42 -> x0, other arithmetic: 12.5 us -> none  [the longest x7 3.56 us: primitive(): GAMMA_LESS * (state[4] - 0.5 * density * jnp.sum(velocity * velocity, axi...]
    div x20 -> x0, other arithmetic: 11.7 us -> none  [the longest x6 5.9 us: face_flux(): turb_right = right_cell[5] / density_right]
  transfers between devices with their start and end apart: 16 -> 0, of which waited for: 0 -> 0; matrix products, arithmetic and copies ran while one was open for 12% -> 0% of each run, Pallas kernels for 0% -> 0%
where the time goes in v1:
time: 41.7 us; the launch traced here: 41.4 us
  Pallas kernels  35.1 us (84%)
  local copies, waits for them, and re-layouts  5.65 us (14%)
  between operations  0.65 us (2%)
    pallas_call x1, Pallas kernels, on_device(): pl.pallas_call(functools.partial(kernel, chord_count, span_count, entries...  35.1 us
    unnamed x11, local copies, waits for them, and re-layouts  5.02 us

profile of v1, /device:TPU:1, one launch (start us, length us, event | category | flops | bytes accessed | tf_op | source)
XLA Modules:
  0.0 41.4 jit_solution(16346237461267277934)
XLA Ops:
  0.6 0.0 copy-start.4
  0.6 0.7 %copy-done.4 = s32[8,128]{1,0:T(8,128)S(1)} copy-done((s32[8,128]{1,0:T(8,128)S(1)}, s32[8,128]{1,0:T(8,128)}, u32[]{:S(2)}) %copy-start.4) | copy-done | bytes 4120
  1.3 0.0 copy-start
  1.3 1.0 %copy-done = f32[6,12,8,128]{3,2,1,0:T(8,128)S(1)} copy-done((f32[6,12,8,128]{3,2,1,0:T(8,128)S(1)}, f32[6,12,8,128]{3,2,1,0:T(8,128)}, u32[]{:S(2)}) %copy-start) | copy-done | bytes 294936
  2.3 0.0 copy-start.1
  2.3 1.0 %copy-done.1 = f32[6,12,8,128]{3,2,1,0:T(8,128)S(1)} copy-done((f32[6,12,8,128]{3,2,1,0:T(8,128)S(1)}, f32[6,12,8,128]{3,2,1,0:T(8,128)}, u32[]{:S(2)}) %copy-start.1) | copy-done | bytes 294936
  3.2 0.0 copy-start.2
  3.2 0.9 %copy-done.2 = f32[3,12,8,128]{3,2,1,0:T(8,128)S(1)} copy-done((f32[3,12,8,128]{3,2,1,0:T(8,128)S(1)}, f32[3,12,8,128]{3,2,1,0:T(8,128)}, u32[]{:S(2)}) %copy-start.2) | copy-done | bytes 147480
  4.2 0.0 copy-start.3
  4.2 0.8 %copy-done.3 = f32[12,8,128]{2,1,0:T(8,128)S(1)} copy-done((f32[12,8,128]{2,1,0:T(8,128)S(1)}, f32[12,8,128]{2,1,0:T(8,128)}, u32[]{:S(2)}) %copy-start.3) | copy-done | bytes 49176
  5.0 35.1 %arnoldi.1 = (f32[6,96,128]{2,1,0:T(8,128)S(1)}, f32[8,128]{1,0:T(8,128)S(1)}) custom-call(f32[6,96,128]{2,1,0:T(8,128)S(1)} %bitcast.5, f32[3,96,128]{2,1,0:T(8,128)S(1)} %bitcast.8, f32[96,128]{1,0:T(8,128)S(1)} %bitcast.9, s32[8,128]{1,0:T(8,128)S(1)} %copy-done.4, f32[6,96,128]{2,1,0:T(8,128)S(1)} %bitcast.6), custom_call_target="tpu_custom_call" | custom-call | tf_op jit(solution)/shard_map/arnoldi/pallas_call | solution.py:582
  40.1 0.6 %slice_reduce_fusion = f32[5]{0:T(128)} fusion(f32[8,128]{1,0:T(8,128)S(1)} %get-tuple-element.5), kind=kLoop, calls=%fused_computation | loop fusion | bytes 40 | tf_op jit(solution)/shard_map/slice | solution.py:616
  40.7 0.7 %copy.8 = f32[6,12,8,128]{3,2,1,0:T(8,128)} copy(f32[6,12,8,128]{3,2,1,0:T(8,128)S(1)} %bitcast.7) | data formatting | bytes 589824
Async XLA Ops:
  0.6 0.7 %copy-start.4 = (s32[8,128]{1,0:T(8,128)S(1)}, s32[8,128]{1,0:T(8,128)}, u32[]{:S(2)}) copy-start(s32[8,128]{1,0:T(8,128)} %codes.1) | copy-start | bytes 12292
  1.3 1.0 %copy-start = (f32[6,12,8,128]{3,2,1,0:T(8,128)S(1)}, f32[6,12,8,128]{3,2,1,0:T(8,128)}, u32[]{:S(2)}) copy-start(f32[6,12,8,128]{3,2,1,0:T(8,128)} %param.5) | copy-start | bytes 884740
  2.3 1.0 %copy-start.1 = (f32[6,12,8,128]{3,2,1,0:T(8,128)S(1)}, f32[6,12,8,128]{3,2,1,0:T(8,128)}, u32[]{:S(2)}) copy-start(f32[6,12,8,128]{3,2,1,0:T(8,128)} %param.9) | copy-start | bytes 884740
  3.2 0.9 %copy-start.2 = (f32[3,12,8,128]{3,2,1,0:T(8,128)S(1)}, f32[3,12,8,128]{3,2,1,0:T(8,128)}, u32[]{:S(2)}) copy-start(f32[3,12,8,128]{3,2,1,0:T(8,128)} %param.6) | copy-start | bytes 442372
  4.2 0.8 %copy-start.3 = (f32[12,8,128]{2,1,0:T(8,128)S(1)}, f32[12,8,128]{2,1,0:T(8,128)}, u32[]{:S(2)}) copy-start(f32[12,8,128]{2,1,0:T(8,128)} %param.7) | copy-start | bytes 147460

commit v2 on v1

--- a/solution.py
+++ b/solution.py
@@ -38,12 +38,12 @@
 RESULT_COUNT = 19
 
 
-def blocks(first, last, size, body):
+def blocks(first, last, size, body, start=0):
     def step(index, carry):
-        body(pl.multiple_of(first + index * size, 8))
-        return carry
-
-    lax.fori_loop(0, (last - first) // size, step, 0)
+        result = body(pl.multiple_of(first + index * size, 8), carry)
+        return carry if result is None else result
+
+    return lax.fori_loop(0, (last - first) // size, step, start)
 
 
 def dot3(a, b):
@@ -57,7 +57,7 @@
 
 
 def slopes_stage(step, first, last, size, window, halves, pulls, prims):
-    def body(row):
+    def body(row, carry):
         here_all = []
         for k in range(6):
             before = window[k, pl.ds(row - step, size), :]
@@ -98,7 +98,7 @@
 
 
 def faces_stage(step, direction, first, last, size, window, offsets, halves, prims, faces):
-    def body(row):
+    def body(row, carry):
         here = pl.ds(row, size)
         after = pl.ds(row + step, size)
         spacing = [offsets[j, after, :] - offsets[j, here, :] for j in range(3)]
@@ -173,7 +173,7 @@
 
 
 def pull_stage(step, first, last, size, vector, faces, results):
-    def body(row):
+    def body(row, carry):
         here = pl.ds(row, size)
         after = pl.ds(row + step, size)
         g = [vector[k, here, :] - vector[k, after, :] for k in range(6)]
@@ -209,8 +209,8 @@
     blocks(first, last, size, body)
 
 
-def cells_stage(step, first, last, size, pulls, prims, results, store, extra=None):
-    def body(row):
+def cells_stage(step, first, last, size, pulls, prims, results, store, extra=None, start=0):
+    def body(row, carry):
         here = pl.ds(row, size)
         before = pl.ds(row - step, size)
         after = pl.ds(row + step, size)
@@ -249,20 +249,22 @@
             outcome[1 + j] = outcome[1 + j] + velocity_bar[j] * inverse
         outcome[4] = outcome[4] + energy_bar * inverse
         outcome[5] = outcome[5] + turbulence_bar * inverse
-        store(row, outcome)
-
-    blocks(first, last, size, body)
+        return store(row, outcome, carry)
+
+    return blocks(first, last, size, body, start)
 
 
 def kernel(
     chord_count, span_count, entries,
-    flow, offset, wall, codes, cost, basis, hessenberg,
+    flow_in, offset_in, wall_in, codes_in, cost_in, m_out, n_out, table,
+    flow, offset, wall, codes, cost,
     wu, wd, wv, cu, cd, cv, su, sd, sv, halves,
     col_pulls, col_prims, col_faces, chord_pulls, chord_prims, chord_faces,
-    span_pulls, span_prims, span_faces, results, source, signs, col_out, chord_out, span_out,
-    mapped, span_sums, chord_sums, send_sem, recv_sem, sum_send, sum_recv,
+    span_pulls, span_prims, span_faces, results, source, signs, col_out, span_out,
+    plain, partial, last, last_plain, sums, load_sem, keep_sem, send_sem, recv_sem, sum_send, sum_recv, hello,
 ):
     chord_id, span_id = lax.axis_index("chord"), lax.axis_index("span")
+    mesh_ids = pl.DeviceIdType.MESH
 
     def chord_at(distance):
         return lax.rem(chord_id + (distance + chord_count), chord_count)
@@ -271,19 +273,33 @@
         return lax.rem(span_id + (distance + span_count), span_count)
 
     barrier = pltpu.get_barrier_semaphore()
-    for d in range(1, chord_count):
-        pl.semaphore_signal(barrier, inc=1, device_id=(chord_at(d), span_id), device_id_type=pl.DeviceIdType.MESH)
-    for d in range(1, span_count):
-        pl.semaphore_signal(barrier, inc=1, device_id=(chord_id, span_at(d)), device_id_type=pl.DeviceIdType.MESH)
-
-    def to_chord_rows(source_ref, target, count):
+    chord_mates = sorted(range(1, chord_count), key=lambda d: min(d, chord_count - d))
+    span_mates = sorted(range(1, span_count), key=lambda d: min(d, span_count - d))
+    mates = [(chord_at(d), span_id) for d in chord_mates[:2]]
+    mates += [(chord_id, span_at(d)) for d in span_mates]
+    mates += [(chord_at(d), span_id) for d in chord_mates[2:]]
+    for mate in mates[:4]:
+        pl.semaphore_signal(barrier, inc=1, device_id=mate, device_id_type=mesh_ids)
+
+    loads = [
+        pltpu.make_async_copy(source_ref, target, load_sem.at[index])
+        for index, (source_ref, target) in enumerate(
+            ((flow_in, flow), (offset_in, offset), (cost_in, cost), (codes_in, codes), (wall_in, wall))
+        )
+    ]
+    for load in loads:
+        load.start()
+    for mate in mates[4:]:
+        pl.semaphore_signal(barrier, inc=1, device_id=mate, device_id_type=mesh_ids)
+
+    def to_chord_rows(source_ref, target, count, first=0, gain=None):
         def body(k, carry):
             for cell in range(CX):
                 base = CHORD_OWN + cell * LAYERS
-                target[k, pl.ds(base, 8), :] = source_ref[k, pl.ds(COL_OWN + cell, 8, stride=CX), :]
-                target[k, pl.ds(base + 8, 4), :] = source_ref[
-                    k, pl.ds(COL_OWN + 8 * CX + cell, 4, stride=CX), :
-                ]
+                high = source_ref[k, pl.ds(first + cell, 8, stride=CX), :]
+                low = source_ref[k, pl.ds(first + 8 * CX + cell, 4, stride=CX), :]
+                target[k, pl.ds(base, 8), :] = high if gain is None else gain * high
+                target[k, pl.ds(base + 8, 4), :] = low if gain is None else gain * low
             return carry
 
         lax.fori_loop(0, count, body, 0)
@@ -319,7 +335,7 @@
                 send_sem=send_sem.at[slot, side],
                 recv_sem=recv_sem.at[slot, side],
                 device_id=target,
-                device_id_type=pl.DeviceIdType.MESH,
+                device_id_type=mesh_ids,
             )
             copy.start()
             copies.append(copy)
@@ -329,6 +345,21 @@
     def arrive(copies):
         for copy in copies:
             copy.wait_recv()
+
+    loads[0].wait()
+    to_chord_rows(flow, cu, 6)
+    loads[1].wait()
+    to_chord_rows(offset, cd, 3)
+    loads[2].wait()
+    to_chord_rows(cost, cv.at[0], 6, gain=0.5)
+    loads[3].wait()
+    loads[4].wait()
+    pl.semaphore_wait(barrier, len(mates))
+    chord_flow = exchange(0, cu, True, 3)
+    chord_offset = exchange(2, cd, True, 2)
+    chord_vector = exchange(4, cv.at[0], True, 2)
+    for d in chord_mates:
+        pl.semaphore_signal(hello, inc=1, device_id=(chord_at(d), span_id), device_id_type=mesh_ids)
 
     own = pl.ds(COL_OWN, ROWS)
     code = codes[...]
@@ -357,22 +388,14 @@
         for layer in range(4):
             wd[j, 128 + 8 * layer : 136 + 8 * layer, :] = top
 
-    to_chord_rows(wu, cu, 6)
     to_span_rows(wu, su, 6)
-    to_chord_rows(wd, cd, 3)
+    span_flow = exchange(1, su, False, 3)
     to_span_rows(wd, sd, 3)
-    to_chord_rows(wv.at[0], cv.at[0], 6)
+    span_offset = exchange(3, sd, False, 2)
     to_span_rows(wv.at[0], sv.at[0], 6)
-
-    pl.semaphore_wait(barrier, chord_count + span_count - 2)
-    chord_flow = exchange(0, cu, True, 3)
-    span_flow = exchange(1, su, False, 3)
-    chord_offset = exchange(2, cd, True, 2)
-    span_offset = exchange(3, sd, False, 2)
-    chord_vector = exchange(4, cv.at[0], True, 2)
     span_vector = exchange(5, sv.at[0], False, 2)
 
-    def source_body(row):
+    def source_body(row, carry):
         here = pl.ds(row, 16)
         cells = pl.ds(row + COL_OWN, 16)
         density = wu[0, cells, :]
@@ -402,7 +425,7 @@
             results[slot, 0:24, :] = jnp.zeros((24, CY), jnp.float32)
         pull_stage(COL_STEP, 24, 136, 16, vector, col_faces, results)
 
-        def ghost_store(row, outcome):
+        def column_store(row, outcome, carry):
             for k in range(6):
                 col_out[k, pl.ds(row, 16), :] = outcome[k]
 
@@ -416,8 +439,8 @@
                 density_bar + source[0, here, :] * value,
             )
 
-        cells_stage(COL_STEP, 16, 32, 16, col_pulls, col_prims, results, ghost_store)
-        cells_stage(COL_STEP, 32, 128, 16, col_pulls, col_prims, results, ghost_store, with_source)
+        cells_stage(COL_STEP, 16, 32, 16, col_pulls, col_prims, results, column_store)
+        cells_stage(COL_STEP, 32, 128, 16, col_pulls, col_prims, results, column_store, with_source)
         for k in range(6):
             sign = signs[k]
             col_out[k, 32:40, :] = col_out[k, 32:40, :] + sign * col_out[k, 24:32, :]
@@ -430,35 +453,36 @@
     def span_product(vector):
         pull_stage(SPAN_STEP, 8, 152, 16, vector, span_faces, results)
 
-        def store(row, outcome):
+        def span_store(row, outcome, carry):
             for k in range(6):
                 span_out[k, pl.ds(pl.multiple_of(row - SPAN_OWN, 8), 16), :] = outcome[k]
 
-        cells_stage(SPAN_STEP, 16, 144, 16, span_pulls, span_prims, results, store)
-
-    def chord_ready():
-        slopes_stage(CHORD_STEP, 16, 160, 16, cu, halves, chord_pulls, chord_prims)
-        faces_stage(CHORD_STEP, 0, 16, 160, 16, cu, cd, halves, chord_prims, chord_faces)
-
-    def chord_product(vector):
+        cells_stage(SPAN_STEP, 16, 144, 16, span_pulls, span_prims, results, span_store)
+
+    def column_and_span():
+        def body(k, carry):
+            plain[k] = span_out[k].T[0:ROWS, :] + col_out[k, own, :]
+            return carry
+
+        lax.fori_loop(0, 6, body, 0)
+        to_chord_rows(plain, partial, 6)
+
+    def chord_product(vector, store, start=0):
         pull_stage(CHORD_STEP, 16, 160, 16, vector, chord_faces, results)
 
-        def store(row, outcome):
-            for k in range(6):
-                chord_out[k, pl.ds(pl.multiple_of(row - CHORD_OWN, 8), 16), :] = outcome[k]
-
-        cells_stage(CHORD_STEP, 40, 136, 16, chord_pulls, chord_prims, results, store)
-
-    def combine(target, halved):
+        def add_store(row, outcome, carry):
+            here = pl.ds(row, 16)
+            return store(row, [outcome[k] + partial[k, here, :] for k in range(6)], carry)
+
+        return cells_stage(
+            CHORD_STEP, 40, 136, 16, chord_pulls, chord_prims, results, add_store, None, start
+        )
+
+    def from_chord_rows(source_ref, target, first):
         def body(k, carry):
-            turned = span_out[k].T
             for layer in range(LAYERS):
-                rows = slice(layer * CX, layer * CX + CX)
-                value = turned[rows, :] + col_out[k, COL_OWN + layer * CX : COL_OWN + layer * CX + CX, :]
-                value = value + chord_out[k, pl.ds(layer, CX, stride=LAYERS), :]
-                mapped[target, k, rows, :] = value
-                if halved:
-                    wv[1, k, COL_OWN + layer * CX : COL_OWN + layer * CX + CX, :] = 0.5 * value
+                rows = pl.ds(CHORD_OWN + layer, CX, stride=LAYERS)
+                target[k, pl.ds(first + layer * CX, CX), :] = source_ref[k, rows, :]
             return carry
 
         lax.fori_loop(0, 6, body, 0)
@@ -469,69 +493,90 @@
     span_ready()
     arrive(span_vector)
     span_product(sv.at[0])
-    arrive(chord_flow + chord_offset)
-    chord_ready()
+    column_and_span()
+    arrive(chord_flow)
+    slopes_stage(CHORD_STEP, 16, 160, 16, cu, halves, chord_pulls, chord_prims)
+    arrive(chord_offset)
+    faces_stage(CHORD_STEP, 0, 16, 160, 16, cu, cd, halves, chord_prims, chord_faces)
     arrive(chord_vector)
-    chord_product(cv.at[0])
-    combine(0, True)
-
-    to_chord_rows(wv.at[1], cv.at[1], 6)
+
+    def first_store(row, outcome, carry):
+        for k in range(6):
+            cv[1, k, pl.ds(row, 16), :] = 0.5 * outcome[k]
+
+    chord_product(cv.at[0], first_store)
+
     chord_vector = exchange(6, cv.at[1], True, 2)
+    from_chord_rows(cv.at[1], wv.at[1], COL_OWN)
     to_span_rows(wv.at[1], sv.at[1], 6)
     span_vector = exchange(7, sv.at[1], False, 2)
-
-    def inner(pairs):
-        def body(k, sums):
-            sums = list(sums)
-            for layer in range(LAYERS):
-                rows = slice(layer * CX, layer * CX + CX)
-                values = [cost[k, rows, :], mapped[0, k, rows, :], mapped[1, k, rows, :]]
-                for index, (one, two) in enumerate(pairs):
-                    sums[index] = sums[index] + values[one] * values[two]
-            return tuple(sums)
-
-        return lax.fori_loop(0, 6, body, tuple(jnp.zeros((CX, CY), jnp.float32) for _ in pairs))
-
-    first_sums = inner(((0, 0), (0, 1), (1, 1)))
+    nothing = jnp.zeros((16, CY), jnp.float32)
+
+    def first_inner(row, carry):
+        cc, cm, mm = carry
+        here = pl.ds(row, 16)
+        for k in range(6):
+            c, m = cv[0, k, here, :], cv[1, k, here, :]
+            cc, cm, mm = cc + c * c, cm + c * m, mm + m * m
+        return cc, cm, mm
+
+    keep_m = pltpu.make_async_copy(wv.at[1, :, own, :], m_out, keep_sem.at[0])
+    keep_m.start()
+    first_sums = blocks(40, 136, 16, first_inner, (nothing,) * 3)
     column_product(wv.at[1])
     arrive(span_vector)
     span_product(sv.at[1])
+    column_and_span()
     arrive(chord_vector)
-    chord_product(cv.at[1])
-    combine(1, False)
-    second_sums = inner(((0, 2), (1, 2), (2, 2)))
+
+    def second_store(row, outcome, carry):
+        cn, mn, nn = carry
+        here = pl.ds(row, 16)
+        for k in range(6):
+            n = 0.5 * outcome[k]
+            last[k, here, :] = n
+            c, m = cv[0, k, here, :], cv[1, k, here, :]
+            cn, mn, nn = cn + c * n, mn + m * n, nn + n * n
+        return cn, mn, nn
+
+    second_sums = chord_product(cv.at[1], second_store, (nothing,) * 3)
 
     row_of = lax.broadcasted_iota(jnp.int32, (8, CY), 0)
+    lane_of = lax.broadcasted_iota(jnp.int32, (8, CY), 1)
     packed = jnp.zeros((8, CY), jnp.float32)
     for index, value in enumerate(first_sums + second_sums):
         packed = jnp.where(row_of == index, jnp.sum(value, axis=0, keepdims=True), packed)
-
-    def total_over(value, buffer, count, me, at, first_slot):
-        buffer[me] = value
-        copies = []
-        for d in range(1, count):
-            copy = pltpu.make_async_remote_copy(
-                src_ref=buffer.at[me],
-                dst_ref=buffer.at[me],
-                send_sem=sum_send.at[first_slot + d],
-                recv_sem=sum_recv.at[first_slot + d],
-                device_id=at(d),
-                device_id_type=pl.DeviceIdType.MESH,
-            )
-            copy.start()
-            copies.append(copy)
-        started.extend(copies)
-        arrive(copies)
-        total = buffer[0]
-        for index in range(1, count):
-            total = total + buffer[index]
-        return total
-
-    packed = total_over(packed, span_sums, span_count, span_id, lambda d: (chord_id, span_at(d)), 0)
-    packed = total_over(packed, chord_sums, chord_count, chord_id, lambda d: (chord_at(d), span_id), span_count)
-    means = jnp.sum(packed, axis=1, keepdims=True) * (1.0 / entries)
-    means = jnp.broadcast_to(means, (8, CY))
-    cc, cm, mm, cn, mn, nn = [means[index : index + 1, :] for index in range(6)]
+    packed = jnp.broadcast_to(jnp.sum(packed, axis=1, keepdims=True), (8, CY))
+    packed = jnp.where((lane_of >= 16 * row_of) & (lane_of < 16 * row_of + 16), packed, 0.0)
+    mine = pl.multiple_of((chord_id * span_count + span_id) * 8, 8)
+    sums[pl.ds(mine, 1), :] = jnp.sum(packed, axis=0, keepdims=True)
+
+    pl.semaphore_wait(hello, chord_count - 1)
+    copies = []
+    for index, (chord_to, span_to) in enumerate(all_partners(chord_count, span_count)):
+        copy = pltpu.make_async_remote_copy(
+            src_ref=sums.at[pl.ds(mine, 1), :],
+            dst_ref=sums.at[pl.ds(mine, 1), :],
+            send_sem=sum_send.at[index],
+            recv_sem=sum_recv.at[index],
+            device_id=(chord_to(chord_id), span_to(span_id)),
+            device_id_type=mesh_ids,
+        )
+        copy.start()
+        copies.append(copy)
+    started.extend(copies)
+    from_chord_rows(last, last_plain, 0)
+    keep_n = pltpu.make_async_copy(last_plain, n_out, keep_sem.at[1])
+    keep_n.start()
+    arrive(copies)
+    spread = min(8, chord_count * span_count)
+    total = sums[pl.ds(0, spread, stride=8), :]
+    for group in range(1, chord_count * span_count // spread):
+        total = total + sums[pl.ds(group * 64, spread, stride=8), :]
+    total = jnp.sum(total, axis=0, keepdims=True) * (4.0 / entries)
+    cc, cm, mm, cn, mn, nn = [
+        jnp.broadcast_to(total[:, 16 * index : 16 * index + 1], (1, CY)) for index in range(6)
+    ]
 
     scale = lax.rsqrt(cc + NORM_EPS)
     h11 = cm * scale * scale
@@ -551,25 +596,73 @@
     square = jnp.maximum(fresh, 0.0) + NORM_EPS
     inverse = lax.rsqrt(square)
     h32 = square * inverse
-    factors = [jnp.broadcast_to(f * inverse, (CX, CY)) for f in (along_c, along_m, gain)]
-    entries_out = jnp.zeros((8, CY), jnp.float32)
-    for index, value in enumerate((h11, h21, h12, h22, h32)):
-        entries_out = jnp.where(row_of == index, value, entries_out)
-    hessenberg[...] = entries_out
-
-    def final_body(k, carry):
-        for layer in range(LAYERS):
-            rows = slice(layer * CX, layer * CX + CX)
-            basis[k, rows, :] = (
-                factors[0] * cost[k, rows, :]
-                + factors[1] * mapped[0, k, rows, :]
-                + factors[2] * mapped[1, k, rows, :]
-            )
-        return carry
-
-    lax.fori_loop(0, 6, final_body, 0)
+    factors = [f * inverse for f in (along_c, 2.0 * along_m, 2.0 * gain)]
+    rows_out = jnp.zeros((8, CY), jnp.float32)
+    for index, value in enumerate((h11, h21, h12, h22, h32) + tuple(factors)):
+        rows_out = jnp.where(row_of == index, value, rows_out)
+    table[...] = rows_out
     for copy in started:
         copy.wait_send()
+    keep_m.wait()
+    keep_n.wait()
+
+
+def all_partners(chord_count, span_count):
+    ys = min(4, chord_count)
+    zh = chord_count // ys
+    cores = min(2, span_count)
+    zl = min(2, span_count // cores)
+    xs = span_count // (cores * zl)
+
+    def chord_to(dz, dy):
+        return lambda c: lax.rem(lax.div(c, ys) + dz, zh) * ys + lax.rem(c + dy, ys)
+
+    def span_to(dx, dz, dk):
+        def place(s):
+            x = lax.rem(lax.div(s, zl * cores) + dx, xs)
+            z = lax.rem(lax.div(s, cores) + dz, zl)
+            return (x * zl + z) * cores + lax.rem(s + dk, cores)
+
+        return place
+
+    found = []
+    for high in range(zh):
+        for dy in range(ys):
+            for dx in range(xs):
+                for low in range(zl):
+                    for dk in range(cores):
+                        hops = min(dy, ys - dy) + min(dx, xs - dx) + (2 if high > low else low)
+                        if high + dy + dx + low + dk:
+                            found.append((hops, chord_to(high, dy), span_to(dx, low, dk)))
+    found.sort(key=lambda entry: -entry[0])
+    return [entry[1:] for entry in found]
+
+
+def final_kernel(
+    table_in, cost_in, m_in, n_in, basis_out, hessenberg, cost, m, n, table, basis, load_sem, out_sem
+):
+    loads = [
+        pltpu.make_async_copy(source_ref, target, load_sem.at[index])
+        for index, (source_ref, target) in enumerate(
+            ((table_in, table), (cost_in, cost), (m_in, m), (n_in, n))
+        )
+    ]
+    for load in loads:
+        load.start()
+    loads[0].wait()
+    factors = [jnp.broadcast_to(table[row : row + 1, :], (ROWS, CY)) for row in (5, 6, 7)]
+    for index in range(5):
+        hessenberg[index] = table[index, 0]
+    for load in loads[1:]:
+        load.wait()
+    stores = []
+    for k in range(6):
+        basis[k] = factors[0] * cost[k] + factors[1] * m[k] + factors[2] * n[k]
+        store = pltpu.make_async_copy(basis.at[k], basis_out.at[k], out_sem.at[k])
+        store.start()
+        stores.append(store)
+    for store in stores:
+        store.wait()
 
 
 def on_device(chord_count, span_count, flow_state, displacement, wall_distance, face_codes, cost_gradient):
@@ -579,15 +672,20 @@
         return pltpu.VMEM(shape, jnp.float32)
 
     whole = pl.BlockSpec(memory_space=pltpu.VMEM)
-    basis, table = pl.pallas_call(
+    outside = pl.BlockSpec(memory_space=pl.ANY)
+    devices = chord_count * span_count
+    m, n, table = pl.pallas_call(
         functools.partial(kernel, chord_count, span_count, entries),
         out_shape=(
             jax.ShapeDtypeStruct((6, ROWS, CY), jnp.float32),
+            jax.ShapeDtypeStruct((6, ROWS, CY), jnp.float32),
             jax.ShapeDtypeStruct((8, CY), jnp.float32),
         ),
-        in_specs=[whole] * 5,
-        out_specs=(whole, whole),
+        in_specs=[outside] * 5,
+        out_specs=(outside, outside, whole),
         scratch_shapes=[
+            vmem(6, ROWS, CY), vmem(3, ROWS, CY), vmem(ROWS, CY), pltpu.VMEM((CX, CY), jnp.int32),
+            vmem(6, ROWS, CY),
             vmem(6, COL_ROWS, CY), vmem(3, COL_ROWS, CY), vmem(2, 6, COL_ROWS, CY),
             vmem(6, CHORD_ROWS, CY), vmem(3, CHORD_ROWS, CY), vmem(2, 6, CHORD_ROWS, CY),
             vmem(6, SPAN_ROWS, CY), vmem(3, SPAN_ROWS, CY), vmem(2, 6, SPAN_ROWS, CY),
@@ -596,14 +694,16 @@
             vmem(18, CHORD_ROWS, CY), vmem(6, CHORD_ROWS, CY), vmem(FACE_COUNT, CHORD_ROWS, CY),
             vmem(18, SPAN_ROWS, CY), vmem(6, SPAN_ROWS, CY), vmem(FACE_COUNT, SPAN_ROWS, CY),
             vmem(RESULT_COUNT, CHORD_ROWS, CY), vmem(3, ROWS, CY), vmem(6, CX, CY),
-            vmem(6, COL_ROWS, CY), vmem(6, ROWS, CY), vmem(6, CY, CY),
-            vmem(2, 6, ROWS, CY), vmem(span_count, 8, CY), vmem(chord_count, 8, CY),
+            vmem(6, COL_ROWS, CY), vmem(6, CY, CY),
+            vmem(6, ROWS, CY), vmem(6, CHORD_ROWS, CY), vmem(6, CHORD_ROWS, CY), vmem(6, ROWS, CY),
+            vmem(8 * devices, CY),
+            pltpu.SemaphoreType.DMA((5,)), pltpu.SemaphoreType.DMA((2,)),
             pltpu.SemaphoreType.DMA((8, 2)), pltpu.SemaphoreType.DMA((8, 2)),
-            pltpu.SemaphoreType.DMA((span_count + chord_count,)),
-            pltpu.SemaphoreType.DMA((span_count + chord_count,)),
+            pltpu.SemaphoreType.DMA((devices,)), pltpu.SemaphoreType.DMA((devices,)),
+            pltpu.SemaphoreType.REGULAR,
         ],
         compiler_params=pltpu.CompilerParams(
-            collective_id=0, has_side_effects=True, vmem_limit_bytes=48 * 1024 * 1024
+            collective_id=0, has_side_effects=True, vmem_limit_bytes=62 * 1024 * 1024
         ),
         name="arnoldi",
     )(
@@ -613,7 +713,22 @@
         face_codes,
         cost_gradient.reshape(6, ROWS, CY),
     )
-    return basis.reshape(cost_gradient.shape), table[:5, 0]
+    basis, hessenberg = pl.pallas_call(
+        final_kernel,
+        out_shape=(
+            jax.ShapeDtypeStruct((6, ROWS, CY), jnp.float32),
+            jax.ShapeDtypeStruct((5,), jnp.float32),
+        ),
+        in_specs=[outside] * 4,
+        out_specs=(outside, pl.BlockSpec(memory_space=pltpu.SMEM)),
+        scratch_shapes=[
+            vmem(6, ROWS, CY), vmem(6, ROWS, CY), vmem(6, ROWS, CY), vmem(8, CY), vmem(6, ROWS, CY),
+            pltpu.SemaphoreType.DMA((4,)), pltpu.SemaphoreType.DMA((6,)),
+        ],
+        compiler_params=pltpu.CompilerParams(vmem_limit_bytes=62 * 1024 * 1024),
+        name="combination",
+    )(table, cost_gradient.reshape(6, ROWS, CY), m, n)
+    return basis.reshape(cost_gradient.shape), hessenberg
 
 
 def solution(mesh):

time: 41.7 us -> 39.6 us (0.950)
  local copies, waits for them, and re-layouts: 5.65 us -> 0 us
  Pallas kernels: 35.1 us -> 38.8 us
    unnamed x11 -> x0, local copies, waits for them, and re-layouts: 5.02 us -> none
    pallas_call x0 -> x1, Pallas kernels: none -> 2.46 us  [on_device(): pl.pallas_call(final_kernel, out_shape=(jax.ShapeDtypeStruct((6, ROWS, CY...]
    pallas_call x1, Pallas kernels: 35.1 us -> 36.4 us  [on_device(): pl.pallas_call(functools.partial(kernel, chord_count, span_count, entries...]
    slice x1 -> x0, local copies, waits for them, and re-layouts: 0.63 us -> none  [on_device(): return (basis.reshape(cost_gradient.shape), table[:5, 0])]
where the time goes in v2:
time: 39.6 us; the launch traced here: 39.5 us
  Pallas kernels  38.8 us (98%)
  between operations  0.64 us (2%)
    pallas_call x1, Pallas kernels, on_device(): pl.pallas_call(functools.partial(kernel, chord_count, span_count, entries...  36.4 us
    pallas_call x1, Pallas kernels, on_device(): pl.pallas_call(final_kernel, out_shape=(jax.ShapeDtypeStruct((6, ROWS, CY...  2.46 us

profile of v2, /device:TPU:1, one launch (start us, length us, event | category | flops | bytes accessed | tf_op | source)
XLA Modules:
  0.0 39.5 jit_solution(3927360738234759118)
XLA Ops:
  0.6 36.4 %arnoldi.1 = (f32[6,96,128]{2,1,0:T(8,128)}, f32[6,96,128]{2,1,0:T(8,128)}, f32[8,128]{1,0:T(8,128)}) custom-call(f32[6,96,128]{2,1,0:T(8,128)} %bitcast.7, f32[3,96,128]{2,1,0:T(8,128)} %bitcast.8, f32[96,128]{1,0:T(8,128)} %bitcast.9, s32[8,128]{1,0:T(8,128)} %codes_in.1, f32[6,96,128]{2,1,0:T(8,128)} %bitcast.5), custom_call_target="tpu_custom_call" | custom-call | tf_op jit(solution)/shard_map/arnoldi/pallas_call | solution.py:677
  37.0 2.5 %combination.1 = (f32[6,96,128]{2,1,0:T(8,128)}, f32[5]{0:T(128)}) custom-call(f32[8,128]{1,0:T(8,128)} %get-tuple-element.7.table_in, f32[6,96,128]{2,1,0:T(8,128)} %bitcast.6, f32[6,96,128]{2,1,0:T(8,128)} %get-tuple-element.8.m_in, f32[6,96,128]{2,1,0:T(8,128)} %get-tuple-element.9.n_in), custom_call_target="tpu_custom_call" | custom-call | tf_op jit(solution)/shard_map/combination/pallas_call | solution.py:716

commit v3 on v2

--- a/solution.py
+++ b/solution.py
@@ -38,12 +38,18 @@
 RESULT_COUNT = 19
 
 
-def blocks(first, last, size, body, start=0):
+def blocks(first, last, size, body, start=0, gap=None):
+    before = ((gap[0] if gap else last) - first) // size
+    after = (last - gap[1]) // size if gap else 0
+
     def step(index, carry):
-        result = body(pl.multiple_of(first + index * size, 8), carry)
+        row = first + index * size
+        if gap:
+            row = row + lax.div(index, before) * (gap[1] - gap[0])
+        result = body(pl.multiple_of(row, 8 if first % 8 == 0 else 4), carry)
         return carry if result is None else result
 
-    return lax.fori_loop(0, (last - first) // size, step, start)
+    return lax.fori_loop(0, before + after, step, start)
 
 
 def dot3(a, b):
@@ -172,7 +178,7 @@
     return result
 
 
-def pull_stage(step, first, last, size, vector, faces, results):
+def pull_stage(step, first, last, size, vector, faces, results, gap=None):
     def body(row, carry):
         here = pl.ds(row, size)
         after = pl.ds(row + step, size)
@@ -206,10 +212,10 @@
         results[TR, here, :] = shift - diffused
         results[RB, here, :] = faces[FTH, here, :] * mixed_bar
 
-    blocks(first, last, size, body)
-
-
-def cells_stage(step, first, last, size, pulls, prims, results, store, extra=None, start=0):
+    blocks(first, last, size, body, gap=gap)
+
+
+def cells_stage(step, first, last, size, pulls, prims, results, store, extra=None, start=0, gap=None):
     def body(row, carry):
         here = pl.ds(row, size)
         before = pl.ds(row - step, size)
@@ -251,7 +257,7 @@
         outcome[5] = outcome[5] + turbulence_bar * inverse
         return store(row, outcome, carry)
 
-    return blocks(first, last, size, body, start)
+    return blocks(first, last, size, body, start, gap)
 
 
 def kernel(
@@ -261,7 +267,7 @@
     wu, wd, wv, cu, cd, cv, su, sd, sv, halves,
     col_pulls, col_prims, col_faces, chord_pulls, chord_prims, chord_faces,
     span_pulls, span_prims, span_faces, results, source, signs, col_out, span_out,
-    plain, partial, last, last_plain, sums, load_sem, keep_sem, send_sem, recv_sem, sum_send, sum_recv, hello,
+    plain, partial, last, last_plain, sums, others, load_sem, keep_sem, send_sem, recv_sem, sum_send, sum_recv, hello,
 ):
     chord_id, span_id = lax.axis_index("chord"), lax.axis_index("span")
     mesh_ids = pl.DeviceIdType.MESH
@@ -309,7 +315,7 @@
             target[k, pl.ds(SPAN_OWN, CY), :] = source_ref[k, pl.ds(COL_OWN, CY), :].T
             return carry
 
-        lax.fori_loop(0, count, body, 0)
+        lax.fori_loop(0, count, body, 0, unroll=count)
 
     started = []
 
@@ -348,16 +354,16 @@
 
     loads[0].wait()
     to_chord_rows(flow, cu, 6)
+    pl.semaphore_wait(barrier, len(mates))
+    chord_flow = exchange(0, cu, True, 3)
     loads[1].wait()
     to_chord_rows(offset, cd, 3)
+    chord_offset = exchange(2, cd, True, 2)
     loads[2].wait()
     to_chord_rows(cost, cv.at[0], 6, gain=0.5)
+    chord_vector = exchange(4, cv.at[0], True, 2)
     loads[3].wait()
     loads[4].wait()
-    pl.semaphore_wait(barrier, len(mates))
-    chord_flow = exchange(0, cu, True, 3)
-    chord_offset = exchange(2, cd, True, 2)
-    chord_vector = exchange(4, cv.at[0], True, 2)
     for d in chord_mates:
         pl.semaphore_signal(hello, inc=1, device_id=(chord_at(d), span_id), device_id_type=mesh_ids)
 
@@ -464,19 +470,28 @@
             plain[k] = span_out[k].T[0:ROWS, :] + col_out[k, own, :]
             return carry
 
-        lax.fori_loop(0, 6, body, 0)
+        lax.fori_loop(0, 6, body, 0, unroll=6)
         to_chord_rows(plain, partial, 6)
 
-    def chord_product(vector, store, start=0):
-        pull_stage(CHORD_STEP, 16, 160, 16, vector, chord_faces, results)
-
+    def chord_product(vector, arrivals, store, start=0):
         def add_store(row, outcome, carry):
-            here = pl.ds(row, 16)
+            here = pl.ds(row, outcome[0].shape[0])
             return store(row, [outcome[k] + partial[k, here, :] for k in range(6)], carry)
 
-        return cells_stage(
-            CHORD_STEP, 40, 136, 16, chord_pulls, chord_prims, results, add_store, None, start
-        )
+        def some_faces(first, last, size, gap=None):
+            pull_stage(CHORD_STEP, first, last, size, vector, chord_faces, results, gap)
+
+        def some_cells(first, last, size, start, gap=None):
+            return cells_stage(
+                CHORD_STEP, first, last, size, chord_pulls, chord_prims, results, add_store, None, start, gap
+            )
+
+        some_faces(40, 120, 16)
+        some_faces(116, 124, 8)
+        start = some_cells(64, 112, 16, start)
+        arrive(arrivals)
+        some_faces(16, 152, 16, (48, 120))
+        return some_cells(40, 136, 24, start, (64, 112))
 
     def from_chord_rows(source_ref, target, first):
         def body(k, carry):
@@ -498,77 +513,81 @@
     slopes_stage(CHORD_STEP, 16, 160, 16, cu, halves, chord_pulls, chord_prims)
     arrive(chord_offset)
     faces_stage(CHORD_STEP, 0, 16, 160, 16, cu, cd, halves, chord_prims, chord_faces)
-    arrive(chord_vector)
 
     def first_store(row, outcome, carry):
         for k in range(6):
-            cv[1, k, pl.ds(row, 16), :] = 0.5 * outcome[k]
-
-    chord_product(cv.at[0], first_store)
+            cv[1, k, pl.ds(row, outcome[k].shape[0]), :] = 0.5 * outcome[k]
+
+    chord_product(cv.at[0], chord_vector, first_store)
 
     chord_vector = exchange(6, cv.at[1], True, 2)
     from_chord_rows(cv.at[1], wv.at[1], COL_OWN)
     to_span_rows(wv.at[1], sv.at[1], 6)
     span_vector = exchange(7, sv.at[1], False, 2)
-    nothing = jnp.zeros((16, CY), jnp.float32)
+    nothing = jnp.zeros((8, CY), jnp.float32)
+
+    def add_product(total, one, two):
+        product = one * two
+        for part in range(0, product.shape[0], 8):
+            total = total + product[part : part + 8, :]
+        return total
 
     def first_inner(row, carry):
         cc, cm, mm = carry
         here = pl.ds(row, 16)
         for k in range(6):
             c, m = cv[0, k, here, :], cv[1, k, here, :]
-            cc, cm, mm = cc + c * c, cm + c * m, mm + m * m
+            cc, cm, mm = add_product(cc, c, c), add_product(cm, c, m), add_product(mm, m, m)
         return cc, cm, mm
+
+    row_of = lax.broadcasted_iota(jnp.int32, (8, CY), 0)
+    lane_of = lax.broadcasted_iota(jnp.int32, (8, CY), 1)
+
+    def pack(packed, first, values):
+        for index, value in enumerate(values):
+            packed = jnp.where(row_of == first + index, jnp.sum(value, axis=0, keepdims=True), packed)
+        return packed
 
     keep_m = pltpu.make_async_copy(wv.at[1, :, own, :], m_out, keep_sem.at[0])
     keep_m.start()
-    first_sums = blocks(40, 136, 16, first_inner, (nothing,) * 3)
+    packed = pack(nothing, 0, blocks(40, 136, 16, first_inner, (nothing,) * 3))
     column_product(wv.at[1])
     arrive(span_vector)
     span_product(sv.at[1])
     column_and_span()
-    arrive(chord_vector)
 
     def second_store(row, outcome, carry):
         cn, mn, nn = carry
-        here = pl.ds(row, 16)
+        here = pl.ds(row, outcome[0].shape[0])
         for k in range(6):
             n = 0.5 * outcome[k]
             last[k, here, :] = n
             c, m = cv[0, k, here, :], cv[1, k, here, :]
-            cn, mn, nn = cn + c * n, mn + m * n, nn + n * n
+            cn, mn, nn = add_product(cn, c, n), add_product(mn, m, n), add_product(nn, n, n)
         return cn, mn, nn
 
-    second_sums = chord_product(cv.at[1], second_store, (nothing,) * 3)
-
-    row_of = lax.broadcasted_iota(jnp.int32, (8, CY), 0)
-    lane_of = lax.broadcasted_iota(jnp.int32, (8, CY), 1)
-    packed = jnp.zeros((8, CY), jnp.float32)
-    for index, value in enumerate(first_sums + second_sums):
-        packed = jnp.where(row_of == index, jnp.sum(value, axis=0, keepdims=True), packed)
+    packed = pack(packed, 3, chord_product(cv.at[1], chord_vector, second_store, (nothing,) * 3))
+
     packed = jnp.broadcast_to(jnp.sum(packed, axis=1, keepdims=True), (8, CY))
     packed = jnp.where((lane_of >= 16 * row_of) & (lane_of < 16 * row_of + 16), packed, 0.0)
     mine = pl.multiple_of((chord_id * span_count + span_id) * 8, 8)
     sums[pl.ds(mine, 1), :] = jnp.sum(packed, axis=0, keepdims=True)
 
     pl.semaphore_wait(hello, chord_count - 1)
-    copies = []
-    for index, (chord_to, span_to) in enumerate(all_partners(chord_count, span_count)):
+    for chord_to, span_to in all_partners(chord_count, span_count):
         copy = pltpu.make_async_remote_copy(
             src_ref=sums.at[pl.ds(mine, 1), :],
             dst_ref=sums.at[pl.ds(mine, 1), :],
-            send_sem=sum_send.at[index],
-            recv_sem=sum_recv.at[index],
+            send_sem=sum_send,
+            recv_sem=sum_recv,
             device_id=(chord_to(chord_id), span_to(span_id)),
             device_id_type=mesh_ids,
         )
         copy.start()
-        copies.append(copy)
-    started.extend(copies)
     from_chord_rows(last, last_plain, 0)
     keep_n = pltpu.make_async_copy(last_plain, n_out, keep_sem.at[1])
     keep_n.start()
-    arrive(copies)
+    pltpu.make_async_copy(others, others, sum_recv).wait()
     spread = min(8, chord_count * span_count)
     total = sums[pl.ds(0, spread, stride=8), :]
     for group in range(1, chord_count * span_count // spread):
@@ -601,6 +620,7 @@
     for index, value in enumerate((h11, h21, h12, h22, h32) + tuple(factors)):
         rows_out = jnp.where(row_of == index, value, rows_out)
     table[...] = rows_out
+    pltpu.make_async_copy(others, others, sum_send).wait()
     for copy in started:
         copy.wait_send()
     keep_m.wait()
@@ -639,28 +659,28 @@
 
 
 def final_kernel(
-    table_in, cost_in, m_in, n_in, basis_out, hessenberg, cost, m, n, table, basis, load_sem, out_sem
+    table_in, cost_in, m_in, n_in, basis_out, hessenberg, cost, m, n, table, basis, table_sem, load_sem, out_sem
 ):
-    loads = [
-        pltpu.make_async_copy(source_ref, target, load_sem.at[index])
-        for index, (source_ref, target) in enumerate(
-            ((table_in, table), (cost_in, cost), (m_in, m), (n_in, n))
-        )
-    ]
-    for load in loads:
-        load.start()
-    loads[0].wait()
+    first = pltpu.make_async_copy(table_in, table, table_sem)
+    first.start()
+    loads = []
+    for k in range(6):
+        for index, (source_ref, target) in enumerate(((cost_in, cost), (m_in, m), (n_in, n))):
+            load = pltpu.make_async_copy(source_ref.at[k], target.at[k], load_sem.at[k, index])
+            load.start()
+            loads.append(load)
+    first.wait()
     factors = [jnp.broadcast_to(table[row : row + 1, :], (ROWS, CY)) for row in (5, 6, 7)]
-    for index in range(5):
-        hessenberg[index] = table[index, 0]
-    for load in loads[1:]:
-        load.wait()
     stores = []
     for k in range(6):
+        for load in loads[3 * k : 3 * k + 3]:
+            load.wait()
         basis[k] = factors[0] * cost[k] + factors[1] * m[k] + factors[2] * n[k]
         store = pltpu.make_async_copy(basis.at[k], basis_out.at[k], out_sem.at[k])
         store.start()
         stores.append(store)
+    for index in range(5):
+        hessenberg[index] = table[index, 0]
     for store in stores:
         store.wait()
 
@@ -696,10 +716,10 @@
             vmem(RESULT_COUNT, CHORD_ROWS, CY), vmem(3, ROWS, CY), vmem(6, CX, CY),
             vmem(6, COL_ROWS, CY), vmem(6, CY, CY),
             vmem(6, ROWS, CY), vmem(6, CHORD_ROWS, CY), vmem(6, CHORD_ROWS, CY), vmem(6, ROWS, CY),
-            vmem(8 * devices, CY),
+            vmem(8 * devices, CY), vmem(devices - 1, CY),
             pltpu.SemaphoreType.DMA((5,)), pltpu.SemaphoreType.DMA((2,)),
             pltpu.SemaphoreType.DMA((8, 2)), pltpu.SemaphoreType.DMA((8, 2)),
-            pltpu.SemaphoreType.DMA((devices,)), pltpu.SemaphoreType.DMA((devices,)),
+            pltpu.SemaphoreType.DMA, pltpu.SemaphoreType.DMA,
             pltpu.SemaphoreType.REGULAR,
         ],
         compiler_params=pltpu.CompilerParams(
@@ -723,7 +743,7 @@
         out_specs=(outside, pl.BlockSpec(memory_space=pltpu.SMEM)),
         scratch_shapes=[
             vmem(6, ROWS, CY), vmem(6, ROWS, CY), vmem(6, ROWS, CY), vmem(8, CY), vmem(6, ROWS, CY),
-            pltpu.SemaphoreType.DMA((4,)), pltpu.SemaphoreType.DMA((6,)),
+            pltpu.SemaphoreType.DMA, pltpu.SemaphoreType.DMA((6, 3)), pltpu.SemaphoreType.DMA((6,)),
         ],
         compiler_params=pltpu.CompilerParams(vmem_limit_bytes=62 * 1024 * 1024),
         name="combination",

time: 39.6 us -> 36.4 us (0.919)
  Pallas kernels: 38.8 us -> 35.6 us
    pallas_call x1, Pallas kernels: 36.4 us -> 33 us  [on_device(): pl.pallas_call(functools.partial(kernel, chord_count, span_count, entries...]
where the time goes in v3:
time: 36.4 us; the launch traced here: 36.2 us
  Pallas kernels  35.6 us (98%)
  between operations  0.64 us (2%)
    pallas_call x1, Pallas kernels, on_device(): pl.pallas_call(functools.partial(kernel, chord_count, span_count, entries...  33 us
    pallas_call x1, Pallas kernels, on_device(): pl.pallas_call(final_kernel, out_shape=(jax.ShapeDtypeStruct((6, ROWS, CY...  2.53 us

profile of v3, /device:TPU:1, one launch (start us, length us, event | category | flops | bytes accessed | tf_op | source)
XLA Modules:
  0.0 36.2 jit_solution(8385328528032688233)
XLA Ops:
  0.6 33.0 %arnoldi.1 = (f32[6,96,128]{2,1,0:T(8,128)}, f32[6,96,128]{2,1,0:T(8,128)}, f32[8,128]{1,0:T(8,128)}) custom-call(f32[6,96,128]{2,1,0:T(8,128)} %bitcast.7, f32[3,96,128]{2,1,0:T(8,128)} %bitcast.8, f32[96,128]{1,0:T(8,128)} %bitcast.9, s32[8,128]{1,0:T(8,128)} %codes_in.1, f32[6,96,128]{2,1,0:T(8,128)} %bitcast.5), custom_call_target="tpu_custom_call" | custom-call | tf_op jit(solution)/shard_map/arnoldi/pallas_call | solution.py:697
  33.7 2.5 %combination.1 = (f32[6,96,128]{2,1,0:T(8,128)}, f32[5]{0:T(128)}) custom-call(f32[8,128]{1,0:T(8,128)} %get-tuple-element.7.table_in, f32[6,96,128]{2,1,0:T(8,128)} %bitcast.6, f32[6,96,128]{2,1,0:T(8,128)} %get-tuple-element.8.m_in, f32[6,96,128]{2,1,0:T(8,128)} %get-tuple-element.9.n_in), custom_call_target="tpu_custom_call" | custom-call | tf_op jit(solution)/shard_map/combination/pallas_call | solution.py:736

commit v4 on v3

--- a/solution.py
+++ b/solution.py
@@ -352,20 +352,11 @@
         for copy in copies:
             copy.wait_recv()
 
-    loads[0].wait()
+    for load in loads:
+        load.wait()
     to_chord_rows(flow, cu, 6)
-    pl.semaphore_wait(barrier, len(mates))
-    chord_flow = exchange(0, cu, True, 3)
-    loads[1].wait()
     to_chord_rows(offset, cd, 3)
-    chord_offset = exchange(2, cd, True, 2)
-    loads[2].wait()
     to_chord_rows(cost, cv.at[0], 6, gain=0.5)
-    chord_vector = exchange(4, cv.at[0], True, 2)
-    loads[3].wait()
-    loads[4].wait()
-    for d in chord_mates:
-        pl.semaphore_signal(hello, inc=1, device_id=(chord_at(d), span_id), device_id_type=mesh_ids)
 
     own = pl.ds(COL_OWN, ROWS)
     code = codes[...]
@@ -395,11 +386,8 @@
             wd[j, 128 + 8 * layer : 136 + 8 * layer, :] = top
 
     to_span_rows(wu, su, 6)
-    span_flow = exchange(1, su, False, 3)
     to_span_rows(wd, sd, 3)
-    span_offset = exchange(3, sd, False, 2)
     to_span_rows(wv.at[0], sv.at[0], 6)
-    span_vector = exchange(5, sv.at[0], False, 2)
 
     def source_body(row, carry):
         here = pl.ds(row, 16)
@@ -503,6 +491,15 @@
         lax.fori_loop(0, 6, body, 0)
 
     column_ready()
+    pl.semaphore_wait(barrier, len(mates))
+    chord_flow = exchange(0, cu, True, 3)
+    chord_offset = exchange(2, cd, True, 2)
+    chord_vector = exchange(4, cv.at[0], True, 2)
+    span_flow = exchange(1, su, False, 3)
+    span_offset = exchange(3, sd, False, 2)
+    span_vector = exchange(5, sv.at[0], False, 2)
+    for d in chord_mates:
+        pl.semaphore_signal(hello, inc=1, device_id=(chord_at(d), span_id), device_id_type=mesh_ids)
     column_product(wv.at[0])
     arrive(span_flow + span_offset)
     span_ready()

time: 36.4 us -> 35.3 us (0.970)
  Pallas kernels: 35.6 us -> 34.4 us
    pallas_call x1, Pallas kernels: 33 us -> 31.9 us  [on_device(): pl.pallas_call(functools.partial(kernel, chord_count, span_count, entries...]
where the time goes in v4:
time: 35.3 us; the launch traced here: 35.1 us
  Pallas kernels  34.4 us (97%)
  between operations  0.64 us (2%)
    pallas_call x1, Pallas kernels, on_device(): pl.pallas_call(functools.partial(kernel, chord_count, span_count, entries...  31.9 us
    pallas_call x1, Pallas kernels, on_device(): pl.pallas_call(final_kernel, out_shape=(jax.ShapeDtypeStruct((6, ROWS, CY...  2.53 us

profile of v4, /device:TPU:1, one launch (start us, length us, event | category | flops | bytes accessed | tf_op | source)
XLA Modules:
  0.0 35.1 jit_solution(12517015016942658587)
XLA Ops:
  0.6 31.9 %arnoldi.1 = (f32[6,96,128]{2,1,0:T(8,128)}, f32[6,96,128]{2,1,0:T(8,128)}, f32[8,128]{1,0:T(8,128)}) custom-call(f32[6,96,128]{2,1,0:T(8,128)} %bitcast.7, f32[3,96,128]{2,1,0:T(8,128)} %bitcast.8, f32[96,128]{1,0:T(8,128)} %bitcast.9, s32[8,128]{1,0:T(8,128)} %codes_in.1, f32[6,96,128]{2,1,0:T(8,128)} %bitcast.5), custom_call_target="tpu_custom_call" | custom-call | tf_op jit(solution)/shard_map/arnoldi/pallas_call | solution.py:694
  32.5 2.5 %combination.1 = (f32[6,96,128]{2,1,0:T(8,128)}, f32[5]{0:T(128)}) custom-call(f32[8,128]{1,0:T(8,128)} %get-tuple-element.7.table_in, f32[6,96,128]{2,1,0:T(8,128)} %bitcast.6, f32[6,96,128]{2,1,0:T(8,128)} %get-tuple-element.8.m_in, f32[6,96,128]{2,1,0:T(8,128)} %get-tuple-element.9.n_in), custom_call_target="tpu_custom_call" | custom-call | tf_op jit(solution)/shard_map/combination/pallas_call | solution.py:733

commit v5 on v4

--- a/solution.py
+++ b/solution.py
@@ -45,7 +45,7 @@
     def step(index, carry):
         row = first + index * size
         if gap:
-            row = row + lax.div(index, before) * (gap[1] - gap[0])
+            row = row + lax.min(lax.div(index, before), 1) * (gap[1] - gap[0])
         result = body(pl.multiple_of(row, 8 if first % 8 == 0 else 4), carry)
         return carry if result is None else result
 
@@ -62,7 +62,7 @@
     return inverse, velocity, state[5] * inverse, state[4] * inverse
 
 
-def slopes_stage(step, first, last, size, window, halves, pulls, prims):
+def slopes_stage(step, first, last, size, window, halves, pulls, prims, gap=None):
     def body(row, carry):
         here_all = []
         for k in range(6):
@@ -93,7 +93,7 @@
         prims[4, rows, :] = turbulence
         prims[5, rows, :] = specific
 
-    blocks(first, last, size, body)
+    blocks(first, last, size, body, gap=gap)
 
 
 def side_coefficients(state, normal):
@@ -103,7 +103,9 @@
     return velocity + [kinetic, specific + pressure_ratio, turbulence, dot3(velocity, normal)]
 
 
-def faces_stage(step, direction, first, last, size, window, offsets, halves, prims, faces):
+def faces_stage(
+    step, direction, first, last, size, window, offsets, halves, prims, faces, gap=None
+):
     def body(row, carry):
         here = pl.ds(row, size)
         after = pl.ds(row + step, size)
@@ -158,7 +160,7 @@
         faces[FRH, here, :] = half_density
         faces[FTH, here, :] = half_turbulence
 
-    blocks(first, last, size, body)
+    blocks(first, last, size, body, gap=gap)
 
 
 def side_pullback(faces, here, base, normal, wave, shared, g):
@@ -262,12 +264,12 @@
 
 def kernel(
     chord_count, span_count, entries,
-    flow_in, offset_in, wall_in, codes_in, cost_in, m_out, n_out, table,
+    flow_in, offset_in, wall_in, codes_in, cost_in, m_out, n_out, sums,
     flow, offset, wall, codes, cost,
     wu, wd, wv, cu, cd, cv, su, sd, sv, halves,
     col_pulls, col_prims, col_faces, chord_pulls, chord_prims, chord_faces,
     span_pulls, span_prims, span_faces, results, source, signs, col_out, span_out,
-    plain, partial, last, last_plain, sums, others, load_sem, keep_sem, send_sem, recv_sem, sum_send, sum_recv, hello,
+    plain, partial, last, last_plain, row, others, load_sem, keep_sem, send_sem, recv_sem, sum_send, sum_recv, hello,
 ):
     chord_id, span_id = lax.axis_index("chord"), lax.axis_index("span")
     mesh_ids = pl.DeviceIdType.MESH
@@ -440,18 +442,29 @@
             col_out[k, 32:40, :] = col_out[k, 32:40, :] + sign * col_out[k, 24:32, :]
             col_out[k, 40:48, :] = col_out[k, 40:48, :] + sign * col_out[k, 16:24, :]
 
-    def span_ready():
-        slopes_stage(SPAN_STEP, 8, 152, 16, su, halves, span_pulls, span_prims)
-        faces_stage(SPAN_STEP, 1, 8, 152, 16, su, sd, halves, span_prims, span_faces)
-
-    def span_product(vector):
-        pull_stage(SPAN_STEP, 8, 152, 16, vector, span_faces, results)
+    def span_ready(first, last, faces_last, gap=None, faces_gap=None):
+        slopes_stage(SPAN_STEP, first, last, 16, su, halves, span_pulls, span_prims, gap)
+        faces_stage(
+            SPAN_STEP, 1, first, faces_last, 16, su, sd, halves, span_prims, span_faces, faces_gap
+        )
+
+    def span_product(vector, first, last, cells_first, cells_last, gap=None, cells_gap=None):
+        pull_stage(SPAN_STEP, first, last, 16, vector, span_faces, results, gap)
 
         def span_store(row, outcome, carry):
             for k in range(6):
                 span_out[k, pl.ds(pl.multiple_of(row - SPAN_OWN, 8), 16), :] = outcome[k]
 
-        cells_stage(SPAN_STEP, 16, 144, 16, span_pulls, span_prims, results, span_store)
+        cells_stage(
+            SPAN_STEP, cells_first, cells_last, 16, span_pulls, span_prims, results, span_store,
+            gap=cells_gap,
+        )
+
+    def span_inside(vector):
+        span_product(vector, 24, 120, 32, 112)
+
+    def span_edges(vector):
+        span_product(vector, 8, 152, 16, 144, (24, 120), (32, 112))
 
     def column_and_span():
         def body(k, carry):
@@ -501,10 +514,12 @@
     for d in chord_mates:
         pl.semaphore_signal(hello, inc=1, device_id=(chord_at(d), span_id), device_id_type=mesh_ids)
     column_product(wv.at[0])
+    span_ready(24, 136, 120)
+    span_inside(sv.at[0])
     arrive(span_flow + span_offset)
-    span_ready()
+    span_ready(8, 152, 152, (24, 136), (24, 120))
     arrive(span_vector)
-    span_product(sv.at[0])
+    span_edges(sv.at[0])
     column_and_span()
     arrive(chord_flow)
     slopes_stage(CHORD_STEP, 16, 160, 16, cu, halves, chord_pulls, chord_prims)
@@ -549,8 +564,9 @@
     keep_m.start()
     packed = pack(nothing, 0, blocks(40, 136, 16, first_inner, (nothing,) * 3))
     column_product(wv.at[1])
+    span_inside(sv.at[1])
     arrive(span_vector)
-    span_product(sv.at[1])
+    span_edges(sv.at[1])
     column_and_span()
 
     def second_store(row, outcome, carry):
@@ -567,14 +583,16 @@
 
     packed = jnp.broadcast_to(jnp.sum(packed, axis=1, keepdims=True), (8, CY))
     packed = jnp.where((lane_of >= 16 * row_of) & (lane_of < 16 * row_of + 16), packed, 0.0)
-    mine = pl.multiple_of((chord_id * span_count + span_id) * 8, 8)
-    sums[pl.ds(mine, 1), :] = jnp.sum(packed, axis=0, keepdims=True)
+    row[...] = jnp.broadcast_to(jnp.sum(packed, axis=0, keepdims=True), (8, CY))
+    mine = sums.at[chord_id * span_count + span_id, pl.ds(0, 1), :]
+    keep_row = pltpu.make_async_copy(row.at[pl.ds(0, 1), :], mine, keep_sem.at[2])
+    keep_row.start()
 
     pl.semaphore_wait(hello, chord_count - 1)
     for chord_to, span_to in all_partners(chord_count, span_count):
         copy = pltpu.make_async_remote_copy(
-            src_ref=sums.at[pl.ds(mine, 1), :],
-            dst_ref=sums.at[pl.ds(mine, 1), :],
+            src_ref=row.at[pl.ds(0, 1), :],
+            dst_ref=mine,
             send_sem=sum_send,
             recv_sem=sum_recv,
             device_id=(chord_to(chord_id), span_to(span_id)),
@@ -585,11 +603,63 @@
     keep_n = pltpu.make_async_copy(last_plain, n_out, keep_sem.at[1])
     keep_n.start()
     pltpu.make_async_copy(others, others, sum_recv).wait()
-    spread = min(8, chord_count * span_count)
-    total = sums[pl.ds(0, spread, stride=8), :]
-    for group in range(1, chord_count * span_count // spread):
-        total = total + sums[pl.ds(group * 64, spread, stride=8), :]
-    total = jnp.sum(total, axis=0, keepdims=True) * (4.0 / entries)
+    pltpu.make_async_copy(others, others, sum_send).wait()
+    for copy in started:
+        copy.wait_send()
+    keep_m.wait()
+    keep_n.wait()
+    keep_row.wait()
+
+
+def all_partners(chord_count, span_count):
+    ys = min(4, chord_count)
+    zh = chord_count // ys
+    cores = min(2, span_count)
+    zl = min(2, span_count // cores)
+    xs = span_count // (cores * zl)
+
+    def chord_to(dz, dy):
+        return lambda c: lax.rem(lax.div(c, ys) + dz, zh) * ys + lax.rem(c + dy, ys)
+
+    def span_to(dx, dz, dk):
+        def place(s):
+            x = lax.rem(lax.div(s, zl * cores) + dx, xs)
+            z = lax.rem(lax.div(s, cores) + dz, zl)
+            return (x * zl + z) * cores + lax.rem(s + dk, cores)
+
+        return place
+
+    found = []
+    for high in range(zh):
+        for dy in range(ys):
+            for dx in range(xs):
+                for low in range(zl):
+                    for dk in range(cores):
+                        hops = min(dy, ys - dy) + min(dx, xs - dx) + (2 if high > low else low)
+                        if high + dy + dx + low + dk:
+                            found.append((hops, chord_to(high, dy), span_to(dx, low, dk)))
+    found.sort(key=lambda entry: -entry[0])
+    return [entry[1:] for entry in found]
+
+
+def final_kernel(
+    entries, sums_in, cost_in, m_in, n_in, basis_out, hessenberg,
+    cost, m, n, sums, table, basis, sums_sem, load_sem, out_sem,
+):
+    first_row = pl.ds(0, 1)
+    first = pltpu.make_async_copy(sums_in.at[:, first_row, :], sums.at[:, first_row, :], sums_sem)
+    first.start()
+    loads = []
+    for k in range(6):
+        for index, (source_ref, target) in enumerate(((cost_in, cost), (m_in, m), (n_in, n))):
+            load = pltpu.make_async_copy(source_ref.at[k], target.at[k], load_sem.at[k, index])
+            load.start()
+            loads.append(load)
+    first.wait()
+    parts = [sums[device, first_row, :] for device in range(sums.shape[0])]
+    while len(parts) > 1:
+        parts = [sum(parts[index : index + 2]) for index in range(0, len(parts), 2)]
+    total = parts[0] * (4.0 / entries)
     cc, cm, mm, cn, mn, nn = [
         jnp.broadcast_to(total[:, 16 * index : 16 * index + 1], (1, CY)) for index in range(6)
     ]
@@ -613,61 +683,12 @@
     inverse = lax.rsqrt(square)
     h32 = square * inverse
     factors = [f * inverse for f in (along_c, 2.0 * along_m, 2.0 * gain)]
+    row_of = lax.broadcasted_iota(jnp.int32, (8, CY), 0)
     rows_out = jnp.zeros((8, CY), jnp.float32)
-    for index, value in enumerate((h11, h21, h12, h22, h32) + tuple(factors)):
+    for index, value in enumerate((h11, h21, h12, h22, h32)):
         rows_out = jnp.where(row_of == index, value, rows_out)
     table[...] = rows_out
-    pltpu.make_async_copy(others, others, sum_send).wait()
-    for copy in started:
-        copy.wait_send()
-    keep_m.wait()
-    keep_n.wait()
-
-
-def all_partners(chord_count, span_count):
-    ys = min(4, chord_count)
-    zh = chord_count // ys
-    cores = min(2, span_count)
-    zl = min(2, span_count // cores)
-    xs = span_count // (cores * zl)
-
-    def chord_to(dz, dy):
-        return lambda c: lax.rem(lax.div(c, ys) + dz, zh) * ys + lax.rem(c + dy, ys)
-
-    def span_to(dx, dz, dk):
-        def place(s):
-            x = lax.rem(lax.div(s, zl * cores) + dx, xs)
-            z = lax.rem(lax.div(s, cores) + dz, zl)
-            return (x * zl + z) * cores + lax.rem(s + dk, cores)
-
-        return place
-
-    found = []
-    for high in range(zh):
-        for dy in range(ys):
-            for dx in range(xs):
-                for low in range(zl):
-                    for dk in range(cores):
-                        hops = min(dy, ys - dy) + min(dx, xs - dx) + (2 if high > low else low)
-                        if high + dy + dx + low + dk:
-                            found.append((hops, chord_to(high, dy), span_to(dx, low, dk)))
-    found.sort(key=lambda entry: -entry[0])
-    return [entry[1:] for entry in found]
-
-
-def final_kernel(
-    table_in, cost_in, m_in, n_in, basis_out, hessenberg, cost, m, n, table, basis, table_sem, load_sem, out_sem
-):
-    first = pltpu.make_async_copy(table_in, table, table_sem)
-    first.start()
-    loads = []
-    for k in range(6):
-        for index, (source_ref, target) in enumerate(((cost_in, cost), (m_in, m), (n_in, n))):
-            load = pltpu.make_async_copy(source_ref.at[k], target.at[k], load_sem.at[k, index])
-            load.start()
-            loads.append(load)
-    first.wait()
-    factors = [jnp.broadcast_to(table[row : row + 1, :], (ROWS, CY)) for row in (5, 6, 7)]
+    factors = [jnp.broadcast_to(factor, (ROWS, CY)) for factor in factors]
     stores = []
     for k in range(6):
         for load in loads[3 * k : 3 * k + 3]:
@@ -688,18 +709,17 @@
     def vmem(*shape):
         return pltpu.VMEM(shape, jnp.float32)
 
-    whole = pl.BlockSpec(memory_space=pltpu.VMEM)
     outside = pl.BlockSpec(memory_space=pl.ANY)
     devices = chord_count * span_count
-    m, n, table = pl.pallas_call(
+    m, n, sums = pl.pallas_call(
         functools.partial(kernel, chord_count, span_count, entries),
         out_shape=(
             jax.ShapeDtypeStruct((6, ROWS, CY), jnp.float32),
             jax.ShapeDtypeStruct((6, ROWS, CY), jnp.float32),
-            jax.ShapeDtypeStruct((8, CY), jnp.float32),
+            jax.ShapeDtypeStruct((devices, 8, CY), jnp.float32),
         ),
         in_specs=[outside] * 5,
-        out_specs=(outside, outside, whole),
+        out_specs=(outside, outside, outside),
         scratch_shapes=[
             vmem(6, ROWS, CY), vmem(3, ROWS, CY), vmem(ROWS, CY), pltpu.VMEM((CX, CY), jnp.int32),
             vmem(6, ROWS, CY),
@@ -713,8 +733,8 @@
             vmem(RESULT_COUNT, CHORD_ROWS, CY), vmem(3, ROWS, CY), vmem(6, CX, CY),
             vmem(6, COL_ROWS, CY), vmem(6, CY, CY),
             vmem(6, ROWS, CY), vmem(6, CHORD_ROWS, CY), vmem(6, CHORD_ROWS, CY), vmem(6, ROWS, CY),
-            vmem(8 * devices, CY), vmem(devices - 1, CY),
-            pltpu.SemaphoreType.DMA((5,)), pltpu.SemaphoreType.DMA((2,)),
+            vmem(8, CY), vmem(devices - 1, CY),
+            pltpu.SemaphoreType.DMA((5,)), pltpu.SemaphoreType.DMA((3,)),
             pltpu.SemaphoreType.DMA((8, 2)), pltpu.SemaphoreType.DMA((8, 2)),
             pltpu.SemaphoreType.DMA, pltpu.SemaphoreType.DMA,
             pltpu.SemaphoreType.REGULAR,
@@ -731,7 +751,7 @@
         cost_gradient.reshape(6, ROWS, CY),
     )
     basis, hessenberg = pl.pallas_call(
-        final_kernel,
+        functools.partial(final_kernel, entries),
         out_shape=(
             jax.ShapeDtypeStruct((6, ROWS, CY), jnp.float32),
             jax.ShapeDtypeStruct((5,), jnp.float32),
@@ -739,12 +759,13 @@
         in_specs=[outside] * 4,
         out_specs=(outside, pl.BlockSpec(memory_space=pltpu.SMEM)),
         scratch_shapes=[
-            vmem(6, ROWS, CY), vmem(6, ROWS, CY), vmem(6, ROWS, CY), vmem(8, CY), vmem(6, ROWS, CY),
+            vmem(6, ROWS, CY), vmem(6, ROWS, CY), vmem(6, ROWS, CY), vmem(devices, 8, CY), vmem(8, CY),
+            vmem(6, ROWS, CY),
             pltpu.SemaphoreType.DMA, pltpu.SemaphoreType.DMA((6, 3)), pltpu.SemaphoreType.DMA((6,)),
         ],
         compiler_params=pltpu.CompilerParams(vmem_limit_bytes=62 * 1024 * 1024),
         name="combination",
-    )(table, cost_gradient.reshape(6, ROWS, CY), m, n)
+    )(sums, cost_gradient.reshape(6, ROWS, CY), m, n)
     return basis.reshape(cost_gradient.shape), hessenberg
 
 

time: 35.3 us -> 34.7 us (0.983)
  Pallas kernels: 34.4 us -> 33.8 us
    pallas_call x1, Pallas kernels: 31.9 us -> 31 us  [on_device(): pl.pallas_call(functools.partial(kernel, chord_count, span_count, entries...]
where the time goes in v5:
time: 34.7 us; the launch traced here: 34.5 us
  Pallas kernels  33.8 us (97%)
  between operations  0.64 us (2%)
    pallas_call x1, Pallas kernels, on_device(): pl.pallas_call(functools.partial(kernel, chord_count, span_count, entries...  31 us
    pallas_call x1, Pallas kernels, on_device(): pl.pallas_call(functools.partial(final_kernel, entries), out_shape=(jax.S...  2.8 us

profile of v5, /device:TPU:1, one launch (start us, length us, event | category | flops | bytes accessed | tf_op | source)
XLA Modules:
  0.0 34.5 jit_solution(11398177445561718132)
XLA Ops:
  0.6 31.0 %arnoldi.1 = (f32[6,96,128]{2,1,0:T(8,128)}, f32[6,96,128]{2,1,0:T(8,128)}, f32[128,8,128]{2,1,0:T(8,128)}) custom-call(f32[6,96,128]{2,1,0:T(8,128)} %bitcast.7, f32[3,96,128]{2,1,0:T(8,128)} %bitcast.8, f32[96,128]{1,0:T(8,128)} %bitcast.9, s32[8,128]{1,0:T(8,128)} %codes_in.1, f32[6,96,128]{2,1,0:T(8,128)} %bitcast.5), custom_call_target="tpu_custom_call" | custom-call | tf_op jit(solution)/shard_map/arnoldi/pallas_call | solution.py:714
  31.7 2.8 %combination.1 = (f32[6,96,128]{2,1,0:T(8,128)}, f32[5]{0:T(128)}) custom-call(f32[128,8,128]{2,1,0:T(8,128)} %get-tuple-element.7.sums_in, f32[6,96,128]{2,1,0:T(8,128)} %bitcast.6, f32[6,96,128]{2,1,0:T(8,128)} %get-tuple-element.8.m_in, f32[6,96,128]{2,1,0:T(8,128)} %get-tuple-element.9.n_in), custom_call_target="tpu_custom_call" | custom-call | tf_op jit(solution)/shard_map/combination/pallas_call | solution.py:753

commit v6 on v5

--- a/solution.py
+++ b/solution.py
@@ -27,6 +27,7 @@
 
 LAYERS, CX, CY = 12, 8, 128
 ROWS = LAYERS * CX
+PADDED = ROWS + CX
 
 COL_STEP, COL_OWN, COL_ROWS = 8, 32, 160
 CHORD_STEP, CHORD_OWN, CHORD_ROWS = 12, 40, 176
@@ -289,10 +290,17 @@
     for mate in mates[:4]:
         pl.semaphore_signal(barrier, inc=1, device_id=mate, device_id_type=mesh_ids)
 
+    block = pl.ds(0, ROWS)
     loads = [
         pltpu.make_async_copy(source_ref, target, load_sem.at[index])
         for index, (source_ref, target) in enumerate(
-            ((flow_in, flow), (offset_in, offset), (cost_in, cost), (codes_in, codes), (wall_in, wall))
+            (
+                (flow_in, flow.at[:, block, :]),
+                (offset_in, offset.at[:, block, :]),
+                (cost_in, cost.at[:, block, :]),
+                (codes_in, codes),
+                (wall_in, wall),
+            )
         )
     ]
     for load in loads:
@@ -370,10 +378,10 @@
         wu[k, 0:16, :] = jnp.full((16, CY), FREESTREAM[k], jnp.float32)
         wu[k, 16:24, :] = sign * far + level
         wu[k, 24:32, :] = sign * near + level
-        wu[k, own, :] = flow[k]
+        wu[k, own, :] = flow[k, block, :]
         wu[k, 128:160, :] = jnp.full((32, CY), FREESTREAM[k], jnp.float32)
         wv[0, k, 0:32, :] = jnp.zeros((32, CY), jnp.float32)
-        wv[0, k, own, :] = 0.5 * cost[k]
+        wv[0, k, own, :] = 0.5 * cost[k, block, :]
         wv[0, k, 128:160, :] = jnp.zeros((32, CY), jnp.float32)
         wv[1, k, 0:32, :] = jnp.zeros((32, CY), jnp.float32)
         wv[1, k, 128:160, :] = jnp.zeros((32, CY), jnp.float32)
@@ -383,7 +391,7 @@
         wd[j, 8:16, :] = far
         wd[j, 16:24, :] = far
         wd[j, 24:32, :] = near
-        wd[j, own, :] = offset[j]
+        wd[j, own, :] = offset[j, block, :]
         for layer in range(4):
             wd[j, 128 + 8 * layer : 136 + 8 * layer, :] = top
 
@@ -468,7 +476,7 @@
 
     def column_and_span():
         def body(k, carry):
-            plain[k] = span_out[k].T[0:ROWS, :] + col_out[k, own, :]
+            plain[k, block, :] = span_out[k].T[0:ROWS, :] + col_out[k, own, :]
             return carry
 
         lax.fori_loop(0, 6, body, 0, unroll=6)
@@ -602,11 +610,11 @@
     from_chord_rows(last, last_plain, 0)
     keep_n = pltpu.make_async_copy(last_plain, n_out, keep_sem.at[1])
     keep_n.start()
-    pltpu.make_async_copy(others, others, sum_recv).wait()
-    pltpu.make_async_copy(others, others, sum_send).wait()
     for copy in started:
         copy.wait_send()
     keep_m.wait()
+    pltpu.make_async_copy(others, others, sum_recv).wait()
+    pltpu.make_async_copy(others, others, sum_send).wait()
     keep_n.wait()
     keep_row.wait()
 
@@ -721,8 +729,8 @@
         in_specs=[outside] * 5,
         out_specs=(outside, outside, outside),
         scratch_shapes=[
-            vmem(6, ROWS, CY), vmem(3, ROWS, CY), vmem(ROWS, CY), pltpu.VMEM((CX, CY), jnp.int32),
-            vmem(6, ROWS, CY),
+            vmem(6, PADDED, CY), vmem(3, PADDED, CY), vmem(ROWS, CY), pltpu.VMEM((CX, CY), jnp.int32),
+            vmem(6, PADDED, CY),
             vmem(6, COL_ROWS, CY), vmem(3, COL_ROWS, CY), vmem(2, 6, COL_ROWS, CY),
             vmem(6, CHORD_ROWS, CY), vmem(3, CHORD_ROWS, CY), vmem(2, 6, CHORD_ROWS, CY),
             vmem(6, SPAN_ROWS, CY), vmem(3, SPAN_ROWS, CY), vmem(2, 6, SPAN_ROWS, CY),
@@ -732,7 +740,7 @@
             vmem(18, SPAN_ROWS, CY), vmem(6, SPAN_ROWS, CY), vmem(FACE_COUNT, SPAN_ROWS, CY),
             vmem(RESULT_COUNT, CHORD_ROWS, CY), vmem(3, ROWS, CY), vmem(6, CX, CY),
             vmem(6, COL_ROWS, CY), vmem(6, CY, CY),
-            vmem(6, ROWS, CY), vmem(6, CHORD_ROWS, CY), vmem(6, CHORD_ROWS, CY), vmem(6, ROWS, CY),
+            vmem(6, PADDED, CY), vmem(6, CHORD_ROWS, CY), vmem(6, CHORD_ROWS, CY), vmem(6, ROWS, CY),
             vmem(8, CY), vmem(devices - 1, CY),
             pltpu.SemaphoreType.DMA((5,)), pltpu.SemaphoreType.DMA((3,)),
             pltpu.SemaphoreType.DMA((8, 2)), pltpu.SemaphoreType.DMA((8, 2)),

time: 34.7 us -> 34.6 us (level)
  no operation moved by 1% of the time
where the time goes in v6:
time: 34.6 us; the launch traced here: 34.4 us
  Pallas kernels  33.8 us (98%)
  between operations  0.64 us (2%)
    pallas_call x1, Pallas kernels, on_device(): pl.pallas_call(functools.partial(kernel, chord_count, span_count, entries...  31 us
    pallas_call x1, Pallas kernels, on_device(): pl.pallas_call(functools.partial(final_kernel, entries), out_shape=(jax.S...  2.8 us

profile of v6, /device:TPU:1, one launch (start us, length us, event | category | flops | bytes accessed | tf_op | source)
XLA Modules:
  0.0 34.4 jit_solution(10945828716689317219)
XLA Ops:
  0.6 31.0 %arnoldi.1 = (f32[6,96,128]{2,1,0:T(8,128)}, f32[6,96,128]{2,1,0:T(8,128)}, f32[128,8,128]{2,1,0:T(8,128)}) custom-call(f32[6,96,128]{2,1,0:T(8,128)} %bitcast.7, f32[3,96,128]{2,1,0:T(8,128)} %bitcast.8, f32[96,128]{1,0:T(8,128)} %bitcast.9, s32[8,128]{1,0:T(8,128)} %codes_in.1, f32[6,96,128]{2,1,0:T(8,128)} %bitcast.5), custom_call_target="tpu_custom_call" | custom-call | tf_op jit(solution)/shard_map/arnoldi/pallas_call | solution.py:722
  31.6 2.8 %combination.1 = (f32[6,96,128]{2,1,0:T(8,128)}, f32[5]{0:T(128)}) custom-call(f32[128,8,128]{2,1,0:T(8,128)} %get-tuple-element.7.sums_in, f32[6,96,128]{2,1,0:T(8,128)} %bitcast.6, f32[6,96,128]{2,1,0:T(8,128)} %get-tuple-element.8.m_in, f32[6,96,128]{2,1,0:T(8,128)} %get-tuple-element.9.n_in), custom_call_target="tpu_custom_call" | custom-call | tf_op jit(solution)/shard_map/combination/pallas_call | solution.py:761
